TPU v7x, 512 devices: a whole 4x4x16 slice. The times are simulated.
512 devices in a mesh: gx: 32 (over z, core), gy: 16 (over x, y).
Axes of the slice: x: 4, y: 4, z: 16, core: 2. Of those that a mesh axis runs over, the one named last changes fastest.
Arguments:
- adjoint_source: float32 [4, 128, 128, 256], P(None, 'gx', 'gy'), may hold values from -60 to 60, as said below
- labels: int32 [128, 128, 256], P('gx', 'gy'), may hold values from 0 to 2
- bv_mask: int32 [128, 128, 256], P('gx', 'gy'), may hold values 0 or 1
- conduct: bfloat16 [4, 128, 128, 256], P(None, 'gx', 'gy'), may hold values from 0.29882812 to 3
- bv_rate: bfloat16 [3, 128, 128, 256], P(None, 'gx', 'gy'), may hold values from 0.5 to 4
Outputs:
- adjoint: float32 [4, 128, 128, 256], P(None, 'gx', 'gy')
- residual: float32 [4, 128, 128, 256], P(None, 'gx', 'gy')
Inputs may be any that keep to these rules, and one draw needn't show every extreme that they name: `adjoint_source`: entries of order one with scales that vary over voxels.
All inputs are finite; a program needn't handle non-finite values. No bound on the sum of `bv_mask` on one device may be relied on, other than what follows from the above.
Results may differ from a plain program's by a relative error of at most 0.029.
Values sent between devices are 32-bit elements; how exact they have to be, the bound alone decides.
No kernel may reach another device: no remote copies, remote signals or barrier semaphores. Data moves between devices by JAX's collectives and lax.ppermute only.
A program may use at most 64 MiB of HBM per device.

v0:
```python
import jax
import jax.numpy as jnp
from jax import lax
from jax.sharding import PartitionSpec as P

ITERS = 3


PHASE = ((1.0, 0.08, 0.08), (1.0, 0.08, 0.08), (0.08, 1.0, 1.0), (0.08, 1.0, 0.08))
SHIFT = (1.0, 0.5, 0.5, 1.0)
WEIGHT = (0.8, 1.0, -1.0, -0.8)
EPS = 1e-12


def with_halo(x, sides, width):
    for axis, dim in sides:
        size, length = (lax.axis_size(axis), x.shape[dim])
        up = [(i, (i + 1) % size) for i in range(size - 1)]
        down = [(j, i) for i, j in up]
        last = lax.slice_in_dim(x, length - width, length, axis=dim)
        leading = lax.slice_in_dim(x, 0, width, axis=dim)
        before = lax.ppermute(last, axis, up)
        after = lax.ppermute(leading, axis, down)
        x = jnp.concatenate([before, x, after], axis=dim)
    return x


def cell_conductance(labels, conduct):
    rows = []
    for field in range(4):
        table = PHASE[field]
        base = jnp.where(labels == 0, table[0], jnp.where(labels == 1, table[1], table[2]))
        rows.append(base * conduct[field].astype(jnp.float32))
    return jnp.stack(rows)


def coupling_rows(bv_rate, bv_mask):
    rates = bv_rate.astype(jnp.float32)
    interface = bv_mask.astype(jnp.float32)
    return jnp.stack([rates[2], -rates[0], rates[0], rates[1]]) * interface[None]


def neighbours(padded):
    return [
        padded[:, 2:, 1:-1, 1:-1],
        padded[:, :-2, 1:-1, 1:-1],
        padded[:, 1:-1, 2:, 1:-1],
        padded[:, 1:-1, :-2, 1:-1],
        padded[:, 1:-1, 1:-1, 2:],
        padded[:, 1:-1, 1:-1, :-2],
    ]


def pad_depth(rimmed):
    return jnp.pad(rimmed, ((0, 0), (0, 0), (0, 0), (1, 1)))


def combine(vector, field_pad, cond_pad, kcell, couple):
    total = jnp.zeros_like(vector)
    for cond_side, field_side in zip(neighbours(cond_pad), neighbours(field_pad)):
        total = total + cond_side * (vector - field_side)
    mixed = (
        WEIGHT[0] * vector[0]
        + WEIGHT[1] * vector[1]
        + WEIGHT[2] * vector[2]
        + WEIGHT[3] * vector[3]
    )
    shift = jnp.stack(
        [jnp.full(vector.shape[1:], SHIFT[field], vector.dtype) for field in range(4)]
    )
    return shift * vector + kcell * total + couple * mixed[None]


def least_squares(columns, beta):
    count = len(columns)
    zero = beta * 0.0
    rows = [
        [columns[col][row] if row <= col + 1 else zero for col in range(count)]
        for row in range(count + 1)
    ]
    target = [beta] + [zero] * count
    for col in range(count):
        upper = rows[col][col]
        lower = rows[col + 1][col]
        radius = jnp.sqrt(upper * upper + lower * lower)
        cosine = upper / radius
        sine = lower / radius
        for other in range(col, count):
            first = rows[col][other]
            second = rows[col + 1][other]
            rows[col][other] = cosine * first + sine * second
            rows[col + 1][other] = -sine * first + cosine * second
        first = target[col]
        second = target[col + 1]
        target[col] = cosine * first + sine * second
        target[col + 1] = -sine * first + cosine * second
    solved = [zero] * count
    for row in range(count - 1, -1, -1):
        value = target[row]
        for other in range(row + 1, count):
            value = value - rows[row][other] * solved[other]
        solved[row] = value / rows[row][row]
    return solved


def finish(basis, columns, beta):
    count = len(columns)
    solved = least_squares(columns, beta)
    adjoint = solved[0] * basis[0]
    for index in range(1, count):
        adjoint = adjoint + solved[index] * basis[index]
    residual = beta * basis[0]
    for row in range(count + 1):
        value = beta * 0.0
        for col in range(count):
            if row <= col + 1:
                value = value + columns[col][row] * solved[col]
        residual = residual - value * basis[row]
    return (adjoint, residual)


def local(adjoint_source, labels, bv_mask, conduct, bv_rate):
    kcell = cell_conductance(labels, conduct)
    couple = coupling_rows(bv_rate, bv_mask)
    cond_pad = pad_depth(with_halo(kcell, (("gx", 1), ("gy", 2)), 1))
    columns = []
    source_sq = lax.psum(jnp.sum(adjoint_source * adjoint_source), ("gx", "gy"))
    beta = jnp.sqrt(source_sq + EPS)
    basis = [adjoint_source / beta]
    first_step = 0
    for step in range(first_step, ITERS):
        vector = basis[step]
        field_pad = pad_depth(with_halo(vector, (("gx", 1), ("gy", 2)), 1))
        image = combine(vector, field_pad, cond_pad, kcell, couple)
        work = image
        projections = []
        for index in range(step + 1):
            weight = lax.psum(jnp.sum(work * basis[index]), ("gx", "gy"))
            projections.append(weight)
            work = work - weight * basis[index]
        length = jnp.sqrt(lax.psum(jnp.sum(work * work), ("gx", "gy")) + EPS)
        columns.append(projections + [length])
        basis.append(work / length)
    return finish(basis, columns, beta)


def solution(mesh):
    return jax.shard_map(
        local,
        mesh=mesh,
        in_specs=(
            P(None, "gx", "gy", None),
            P("gx", "gy", None),
            P("gx", "gy", None),
            P(None, "gx", "gy", None),
            P(None, "gx", "gy", None),
        ),
        out_specs=(P(None, "gx", "gy", None), P(None, "gx", "gy", None)),
        check_vma=False,
    )
```

profile of v0, /device:TPU:1, one launch (start us, length us, event | category | flops | bytes accessed | tf_op | source)
XLA Modules:
  0.0 1105.0 jit_solution(14355436284682183913)
XLA Ops:
  0.6 1.6 multiply_reduce_fusion.9
  2.2 111.0 %psum.70 = f32[]{:T(128)} all-reduce(f32[]{:T(128)} %multiply_reduce_fusion.9), channel_id=1, replica_groups=mesh['gx'=32,'gy'=16] {'gx','gy'}, use_global_device_ids=true, to_apply=%region_1.2 | all-reduce | flops 1 | bytes 8 | tf_op jit(solution)/shard_map/psum | solution.py:127
  114.0 2.7 collective-permute-start.1
  116.7 2.8 collective-permute-start.3
  119.7 1.9 collective-permute-start
  121.6 3.8 collective-permute-start.2
  126.3 1.3 collective-permute-start.5
  127.6 4.0 collective-permute-start.7
  131.7 1.3 collective-permute-start.4
  133.0 4.0 collective-permute-start.6
  139.1 106.3 %psum.71 = f32[]{:T(128)} all-reduce(f32[]{:T(128)} %get-tuple-element.10), channel_id=1, replica_groups=mesh['gx'=32,'gy'=16] {'gx','gy'}, use_global_device_ids=true, to_apply=%region_3.4 | all-reduce | flops 1 | bytes 8 | tf_op jit(solution)/shard_map/psum | solution.py:138
  246.7 98.6 %psum.72 = f32[]{:T(128)} all-reduce(f32[]{:T(128)} %multiply_reduce_fusion.7), channel_id=1, replica_groups=mesh['gx'=32,'gy'=16] {'gx','gy'}, use_global_device_ids=true, to_apply=%region_5.6 | all-reduce | flops 1 | bytes 8 | tf_op jit(solution)/shard_map/psum | solution.py:141
  346.7 2.6 collective-permute-start.8
  349.3 3.6 collective-permute-start.9
  353.9 1.3 collective-permute-start.10
  355.2 4.0 collective-permute-start.11
  361.4 105.4 %psum.73 = f32[]{:T(128)} all-reduce(f32[]{:T(128)} %get-tuple-element.8), channel_id=1, replica_groups=mesh['gx'=32,'gy'=16] {'gx','gy'}, use_global_device_ids=true, to_apply=%region_7.8 | all-reduce | flops 1 | bytes 8 | tf_op jit(solution)/shard_map/psum | solution.py:138
  466.7 1.3 multiply_reduce_fusion.5
  468.1 100.4 %psum.74 = f32[]{:T(128)} all-reduce(f32[]{:T(128)} %multiply_reduce_fusion.5), channel_id=1, replica_groups=mesh['gx'=32,'gy'=16] {'gx','gy'}, use_global_device_ids=true, to_apply=%region_9.10 | all-reduce | flops 1 | bytes 8 | tf_op jit(solution)/shard_map/psum | solution.py:138
  568.5 2.0 multiply_reduce_fusion.4
  570.5 99.3 %psum.75 = f32[]{:T(128)} all-reduce(f32[]{:T(128)} %get-tuple-element.6), channel_id=1, replica_groups=mesh['gx'=32,'gy'=16] {'gx','gy'}, use_global_device_ids=true, to_apply=%region_11.12 | all-reduce | flops 1 | bytes 8 | tf_op jit(solution)/shard_map/psum | solution.py:141
  670.4 2.6 collective-permute-start.12
  673.0 3.6 collective-permute-start.13
  679.4 1.3 collective-permute-start.14
  680.7 4.0 collective-permute-start.15
  688.7 102.3 %psum.76 = f32[]{:T(128)} all-reduce(f32[]{:T(128)} %get-tuple-element.4), channel_id=1, replica_groups=mesh['gx'=32,'gy'=16] {'gx','gy'}, use_global_device_ids=true, to_apply=%region_13.14 | all-reduce | flops 1 | bytes 8 | tf_op jit(solution)/shard_map/psum | solution.py:138
  791.0 1.4 multiply_reduce_fusion.2
  793.0 100.2 %psum.77 = f32[]{:T(128)} all-reduce(f32[]{:T(128)} %multiply_reduce_fusion.2), channel_id=1, replica_groups=mesh['gx'=32,'gy'=16] {'gx','gy'}, use_global_device_ids=true, to_apply=%region_15.16 | all-reduce | flops 1 | bytes 8 | tf_op jit(solution)/shard_map/psum | solution.py:138
  893.2 2.0 multiply_reduce_fusion.1
  895.8 100.0 %psum.78 = f32[]{:T(128)} all-reduce(f32[]{:T(128)} %get-tuple-element.2), channel_id=1, replica_groups=mesh['gx'=32,'gy'=16] {'gx','gy'}, use_global_device_ids=true, to_apply=%region_17.18 | all-reduce | flops 1 | bytes 8 | tf_op jit(solution)/shard_map/psum | solution.py:138
  997.6 99.4 %psum.79 = f32[]{:T(128)} all-reduce(f32[]{:T(128)} %multiply_reduce_fusion), channel_id=1, replica_groups=mesh['gx'=32,'gy'=16] {'gx','gy'}, use_global_device_ids=true, to_apply=%region_19.20 | all-reduce | flops 1 | bytes 8 | tf_op jit(solution)/shard_map/psum | solution.py:141
  1103.7 1.3 multiply_subtract_fusion
  (59 shorter events, 10.8 us)
Async XLA Ops:
  0.6 113.3 %copy-start = (f32[4,4,8,256]{3,2,1,0:T(8,128)S(1)}, f32[4,4,8,256]{3,2,1,0:T(8,128)}, u32[]{:S(2)}) copy-start(f32[4,4,8,256]{3,2,1,0:T(8,128)} %param.5) | copy-start | bytes 393220
  114.0 5.6 copy-start.3
  114.0 5.6 copy-start.4
  114.0 12.2 %collective-permute-start.1 = (f32[4,1,8,256]{3,2,1,0:T(8,128)S(1)}, f32[4,1,8,256]{3,2,1,0:T(8,128)S(1)}, u32[]{:S(2)}, u32[]{:S(2)}) collective-permute-start(f32[4,1,8,256]{3,2,1,0:T(8,128)S(1)} %get-tuple-element.31), channel_id=1, source_target_pairs={{16,0},{32,16},{48,32},{64,48},{80,64},{96,80},{112,96},{128,112},... | collective-permute-start | bytes 98312 | tf_op jit(solution)/shard_map/ppermute | solution.py:23
  116.7 9.5 collective-permute-start.3
  119.7 11.9 %collective-permute-start = (f32[4,1,8,256]{3,2,1,0:T(8,128)S(1)}, f32[4,1,8,256]{3,2,1,0:T(8,128)S(1)}, u32[]{:S(2)}, u32[]{:S(2)}) collective-permute-start(f32[4,1,8,256]{3,2,1,0:T(8,128)S(1)} %get-tuple-element.29), channel_id=1, source_target_pairs={{16,0},{32,16},{48,32},{64,48},{80,64},{96,80},{112,96},{128,112},... | collective-permute-start | bytes 98312 | tf_op jit(solution)/shard_map/ppermute | solution.py:23
  121.6 3.8 copy-start.2
  121.6 10.0 collective-permute-start.2
  125.5 0.8 copy-start.5
  126.3 10.7 collective-permute-start.5
  127.6 9.4 collective-permute-start.7
  131.7 5.7 collective-permute-start.4
  133.0 4.9 collective-permute-start.6
  137.4 0.9 copy-start.1
  346.7 6.2 collective-permute-start.8
  349.3 4.6 collective-permute-start.9
  353.9 5.3 collective-permute-start.10
  355.2 4.9 collective-permute-start.11
  670.4 8.9 collective-permute-start.12
  673.0 6.3 collective-permute-start.13
  679.4 8.0 collective-permute-start.14
  680.7 6.7 collective-permute-start.15
where the time goes:
time: 1110 us
  blocking collectives  1020 us (92%)
  starting transfers between devices  44.7 us (4%)
  between operations  17 us (2%)
  other arithmetic  16.9 us (2%)
    psum x6, blocking collectives, local(): weight = lax.psum(jnp.sum(work * basis[index]), ('gx', 'gy'))  615 us
    psum x3, blocking collectives, local(): length = jnp.sqrt(lax.psum(jnp.sum(work * work), ('gx', 'gy')) + EPS)  297 us
    psum x1, blocking collectives, local(): source_sq = lax.psum(jnp.sum(adjoint_source * adjoint_source), ('gx', 'gy'))  111 us
    ppermute x8, starting transfers between devices, with_halo(): before = lax.ppermute(last, axis, up)  29.7 us
  transfers between devices with their start and end apart: 16, of which 3 were waited for; matrix products, arithmetic and copies ran while one was open for 0% of the time, Pallas kernels for 0%

commit v1 on v0

v1 whole, which is shorter than its diff:
```python
import jax
import jax.numpy as jnp
from jax import lax
from jax.experimental import pallas as pl
from jax.experimental.pallas import tpu as pltpu
from jax.sharding import PartitionSpec as P

PHASE = ((1.0, 0.08, 0.08), (1.0, 0.08, 0.08), (0.08, 1.0, 1.0), (0.08, 1.0, 0.08))
SHIFT = (1.0, 0.5, 0.5, 1.0)
WEIGHT = (0.8, 1.0, -1.0, -0.8)
EPS = 1e-12
F32 = jnp.float32
VMEM = pl.BlockSpec(memory_space=pltpu.VMEM)
TILE = (8, 256)
Y_TILES = 19
X_TILES = 39
PAIRS = [(i, j) for i in range(4) for j in range(i, 4)]


def rows():
    return lax.broadcasted_iota(jnp.int32, TILE, 0)


def roll(tile, by):
    by = by % 8
    return tile if by == 0 else pltpu.roll(tile, by, 0)


def prepare(source, labels, mask, conduct, rate, kcell, couple, to_right, to_left):
    row = rows()
    for x in range(4):
        phase = labels[x]
        for f in range(4):
            t = PHASE[f]
            base = jnp.where(phase == 0, t[0], jnp.where(phase == 1, t[1], t[2]))
            kcell[f, x] = base * conduct[f, x].astype(F32)
        interface = mask[x].astype(F32)
        for f in range(3):
            couple[f, x] = rate[f, x].astype(F32) * interface
    for f in range(8):
        ref = source if f < 4 else kcell
        for k in range(2):
            a, b = ref[f % 4, 2 * k], ref[f % 4, 2 * k + 1]
            to_right[2 * f + k] = jnp.where(row >= 5, a, roll(b, -3))
            to_left[2 * f + k] = jnp.where(row < 3, a, roll(b, 3))
    for f in range(3):
        right, left = couple[f, 0], couple[f, 0]
        for x in range(1, 4):
            right = jnp.where(row >= 8 - 2 * x, right, roll(couple[f, x], -2 * x))
            left = jnp.where(row < 2 * x, left, roll(couple[f, x], 2 * x))
        to_right[16 + f] = right
        to_left[16 + f] = left


def widen(source, kcell, couple, from_left, from_right, rim, crim, to_right, to_left):
    row = rows()
    zero = jnp.zeros(TILE, F32)
    for f in range(8):
        for x in range(4):
            k, b = 2 * f + x // 2, 3 * (x % 2)
            left, right = roll(from_left[k], b), roll(from_right[k], -b)
            rim[f, x] = jnp.where(row < 3, right, jnp.where(row >= 5, left, zero))
    for f in range(3):
        for x in range(4):
            left, right = roll(from_left[16 + f], 2 * x), roll(from_right[16 + f], -2 * x)
            crim[f, x] = jnp.where(row < 2, right, jnp.where(row >= 6, left, zero))
    for out, order in ((to_right, (3, 2, 1)), (to_left, (0, 1, 2))):
        for f in range(8):
            ref = source if f < 4 else kcell
            for d in range(3):
                out[3 * f + d] = ref[f % 4, order[d]]
            out[30 + f] = jnp.where((row == 2) | (row == 3), roll(rim[f, order[1]], 3), rim[f, order[0]])
        for f in range(3):
            for d in range(2):
                out[24 + 2 * f + d] = couple[f, order[d]]
        c = [roll(crim[f, order[0]], 2 * f) for f in range(3)]
        out[38] = jnp.where((row == 0) | (row == 7), c[0], jnp.where(row <= 2, c[1], c[2]))


def krylov(source, kcell, couple, rim, crim, before, after, k1, k2, k3, gram,
           body, edge, cbody, cedge, dbody, dedge, ubody, uedge):
    row = rows()
    lane = lax.broadcasted_iota(jnp.int32, TILE, 1)
    zero = jnp.zeros(TILE, F32)
    for f in range(8):
        ref = source if f < 4 else kcell
        for x in range(4):
            body[f, 3 + x] = ref[f % 4, x]
            edge[f, 3 + x] = rim[f, x]
        for buf, place in ((before, (2, 1, 0)), (after, (7, 8, 9))):
            for d in range(3):
                body[f, place[d]] = buf[3 * f + d]
            t = buf[30 + f]
            edge[f, place[0]] = jnp.where((row < 2) | (row >= 6), t, zero)
            edge[f, place[1]] = jnp.where((row == 0) | (row == 7), roll(t, -3), zero)
            edge[f, place[2]] = zero
    for f in range(3):
        for x in range(4):
            cbody[f, 3 + x] = couple[f, x]
            cedge[f, 3 + x] = crim[f, x]
        for buf, place in ((before, (2, 1)), (after, (7, 8))):
            for d in range(2):
                cbody[f, place[d]] = buf[24 + 2 * f + d]
            cedge[f, place[0]] = jnp.where((row == 0) | (row == 7), roll(buf[38], -2 * f), zero)
            cedge[f, place[1]] = zero

    def along(b, e):
        ub, ue, db, de = roll(b, -1), roll(e, -1), roll(b, 1), roll(e, 1)
        sb = jnp.where(row == 7, ue, ub) + jnp.where(row == 0, de, db)
        se = jnp.where(row == 7, ub, ue) + jnp.where(row == 0, db, de)
        return sb + depth(b), se + depth(e)

    def depth(t):
        up = jnp.where(lane == 255, zero, pltpu.roll(t, 255, 1))
        down = jnp.where(lane == 0, zero, pltpu.roll(t, 1, 1))
        return up + down

    def diagonal(x, _):
        for f in range(4):
            b, e = body[4 + f, x], edge[4 + f, x]
            sb, se = along(b, e)
            sb = sb + (body[4 + f, x - 1] + body[4 + f, x + 1])
            se = se + (edge[4 + f, x - 1] + edge[4 + f, x + 1])
            dbody[f, x] = SHIFT[f] + b * sb
            dedge[f, x] = SHIFT[f] + e * se
        return 0

    lax.fori_loop(1, 9, diagonal, 0)

    def scale(x, _):
        for f in range(4):
            ubody[f, x] = body[f, x] * body[4 + f, x]
            uedge[f, x] = edge[f, x] * edge[4 + f, x]
        return 0

    def mix(v):
        return WEIGHT[0] * (v[0] - v[3]) + (v[1] - v[2])

    def apply(low, high, out):
        lax.fori_loop(low - 1, high + 1, scale, 0)

        def step(x, _):
            vb, ve = [body[f, x] for f in range(4)], [edge[f, x] for f in range(4)]
            mb, me = mix(vb), mix(ve)
            cb = [cbody[f, x] * mb for f in range(3)]
            ce = [cedge[f, x] * me for f in range(3)]
            cb, ce = [cb[2], -cb[0], cb[0], cb[1]], [ce[2], -ce[0], ce[0], ce[1]]
            for f in range(4):
                sb, se = along(ubody[f, x], uedge[f, x])
                sb = sb + (ubody[f, x - 1] + ubody[f, x + 1])
                se = se + (uedge[f, x - 1] + uedge[f, x + 1])
                body[f, x] = dbody[f, x] * vb[f] - body[4 + f, x] * sb + cb[f]
                edge[f, x] = dedge[f, x] * ve[f] - edge[4 + f, x] * se + ce[f]
            return 0

        lax.fori_loop(low, high, step, 0)
        for f in range(4):
            for x in range(4):
                out[f, x] = body[f, 3 + x]

    apply(1, 9, k1)
    apply(2, 8, k2)
    apply(3, 7, k3)

    def inner(x, sums):
        for f in range(4):
            v = [source[f, x], k1[f, x], k2[f, x], k3[f, x]]
            sums = [s + v[i] * v[j] for s, (i, j) in zip(sums, PAIRS)]
        return sums

    sums = lax.fori_loop(0, 4, inner, [zero] * 10)
    place = lax.broadcasted_iota(jnp.int32, (1, 128), 1)
    line = jnp.zeros((1, 128), F32)
    for index, s in enumerate(sums):
        total = jnp.sum(jnp.sum(s, axis=0, keepdims=True), axis=1, keepdims=True)
        line = jnp.where(place == index, total, line)
    gram[...] = line


def least_squares(columns, beta):
    count = len(columns)
    zero = beta * 0.0
    table = [
        [columns[col][r] if r <= col + 1 else zero for col in range(count)]
        for r in range(count + 1)
    ]
    target = [beta] + [zero] * count
    for col in range(count):
        upper, lower = table[col][col], table[col + 1][col]
        radius = jnp.sqrt(upper * upper + lower * lower)
        cosine, sine = upper / radius, lower / radius
        for other in range(col, count):
            first, second = table[col][other], table[col + 1][other]
            table[col][other] = cosine * first + sine * second
            table[col + 1][other] = -sine * first + cosine * second
        first, second = target[col], target[col + 1]
        target[col] = cosine * first + sine * second
        target[col + 1] = -sine * first + cosine * second
    solved = [zero] * count
    for r in range(count - 1, -1, -1):
        value = target[r]
        for other in range(r + 1, count):
            value = value - table[r][other] * solved[other]
        solved[r] = value / table[r][r]
    return solved


def total(terms):
    out = terms[0]
    for t in terms[1:]:
        out = out + t
    return out


def coefficients(g):
    def dot(u, v):
        return total([total([g[i][j] * v[j] for j in range(len(v))]) * u[i] for i in range(len(u))])

    beta = jnp.sqrt(g[0][0] + EPS)
    basis = [[1.0 / beta]]
    columns = []
    for k in range(3):
        z = [beta * 0.0] + basis[k]
        projections = [dot(basis[i], z) for i in range(k + 1)]
        for i in range(k + 1):
            z = [
                z[j] - projections[i] * basis[i][j] if j < len(basis[i]) else z[j]
                for j in range(k + 2)
            ]
        length = jnp.sqrt(jnp.maximum(dot(z, z), 0.0) + EPS)
        columns.append(projections + [length])
        basis.append([t / length for t in z])
    y = least_squares(columns, beta)
    iterate = [total([y[j] * basis[j][i] for j in range(3) if i < len(basis[j])]) for i in range(3)]
    image = [
        total([columns[col][r] * y[col] for col in range(3) if r <= col + 1]) for r in range(4)
    ]
    image[0] = image[0] - beta
    rest = [-total([image[j] * basis[j][i] for j in range(4) if i < len(basis[j])]) for i in range(4)]
    return iterate, rest


def finish(gram, source, k1, k2, k3, adjoint, residual):
    line = gram[0]
    for i in range(1, gram.shape[0]):
        line = line + gram[i]
    g = [[None] * 4 for _ in range(4)]
    for index, (i, j) in enumerate(PAIRS):
        g[i][j] = g[j][i] = line[:, index:index + 1]
    iterate, rest = coefficients(g)
    iterate = [jnp.broadcast_to(t, TILE) for t in iterate]
    rest = [jnp.broadcast_to(t, TILE) for t in rest]
    vectors = (source, k1, k2, k3)
    for f in range(4):
        for x in range(4):
            v = [ref[f, x] for ref in vectors]
            adjoint[f, x] = total([c * t for c, t in zip(iterate, v)])
            residual[f, x] = total([c * t for c, t in zip(rest, v)])


def call(kernel, ins, outs, scratch=()):
    return pl.pallas_call(
        kernel,
        out_shape=[jax.ShapeDtypeStruct(s, F32) for s in outs],
        in_specs=[VMEM] * ins,
        out_specs=[VMEM] * len(outs),
        scratch_shapes=[pltpu.VMEM(s, F32) for s in scratch],
        compiler_params=pltpu.CompilerParams(vmem_limit_bytes=16 * 2**20),
    )


def swap(to_right, to_left, axis):
    size = lax.axis_size(axis)
    up = [(i, i + 1) for i in range(size - 1)]
    down = [(i + 1, i) for i in range(size - 1)]
    return lax.ppermute(to_right, axis, up), lax.ppermute(to_left, axis, down)


def local(source, labels, mask, conduct, rate):
    four, three = (4, 4) + TILE, (3, 4) + TILE
    kcell, couple, to_right, to_left = call(
        prepare, 5, [four, three, (Y_TILES,) + TILE, (Y_TILES,) + TILE]
    )(source, labels, mask, conduct, rate)
    from_left, from_right = swap(to_right, to_left, "gy")
    rim, crim, to_right, to_left = call(
        widen, 5, [(8, 4) + TILE, three, (X_TILES,) + TILE, (X_TILES,) + TILE]
    )(source, kcell, couple, from_left, from_right)
    before, after = swap(to_right, to_left, "gx")
    wide = (4, 10) + TILE
    k1, k2, k3, gram = call(
        krylov,
        7,
        [four, four, four, (1, 128)],
        [(8, 10) + TILE] * 2 + [(3, 10) + TILE] * 2 + [wide] * 4,
    )(source, kcell, couple, rim, crim, before, after)
    for axis in ("gx", "gy"):
        size = lax.axis_size(axis)
        gram = lax.all_to_all(jnp.broadcast_to(gram[None], (size, 1, 128)), axis, 0, 0)
        if axis == "gx":
            gram = jnp.sum(gram, axis=0)
    return tuple(call(finish, 5, [four, four])(gram, source, k1, k2, k3))


def solution(mesh):
    return jax.shard_map(
        local,
        mesh=mesh,
        in_specs=(
            P(None, "gx", "gy", None),
            P("gx", "gy", None),
            P("gx", "gy", None),
            P(None, "gx", "gy", None),
            P(None, "gx", "gy", None),
        ),
        out_specs=(P(None, "gx", "gy", None), P(None, "gx", "gy", None)),
        check_vma=False,
    )
```

time: 1110 us -> 76 us (0.07)
  blocking collectives: 1020 us -> 41 us
  starting transfers between devices: 44.7 us -> 13.8 us
  other arithmetic: 16.9 us -> 0.02 us
  between operations: 17 us -> 0.69 us
    psum x10 -> x0, blocking collectives: 1020 us -> none  [the longest x6 615 us: local(): weight = lax.psum(jnp.sum(work * basis[index]), ('gx', 'gy'))]
    all_to_all x0 -> x2, blocking collectives: none -> 41 us  [local(): lax.all_to_all(jnp.broadcast_to(gram[None], (size, 1, 128)), axis, 0, 0)]
    ppermute x16 -> x4, starting transfers between devices: 44.7 us -> 13.8 us  [swap(): return (lax.ppermute(to_right, axis, up), lax.ppermute(to_left, axis, down))]
    reduce_sum x10 -> x1, other arithmetic: 13.4 us -> 0.02 us  [local(): gram = jnp.sum(gram, axis=0)]
  transfers between devices with their start and end apart: 16 -> 4, of which waited for: 3 -> 4; matrix products, arithmetic and copies ran while one was open for 0% -> 0% of each run, Pallas kernels for 0% -> 0%
where the time goes in v1:
time: 76 us; the launch traced here: 75.5 us
  blocking collectives  41 us (54%)
  starting transfers between devices  13.8 us (18%)
  waiting for transfers between devices  10.3 us (14%)
  Pallas kernels  5.67 us (7%)
  local copies, waits for them, and re-layouts  4.08 us (5%)
    all_to_all x2, blocking collectives, local(): lax.all_to_all(jnp.broadcast_to(gram[None], (size, 1, 128)), axis, 0, 0)  41 us
    ppermute x4, starting transfers between devices, swap(): return (lax.ppermute(to_right, axis, up), lax.ppermute(to_left, axis, down))  13.8 us
    ppermute x4, waiting for transfers between devices, swap(): return (lax.ppermute(to_right, axis, up), lax.ppermute(to_left, axis, down))  10.3 us
    unnamed x12, local copies, waits for them, and re-layouts  4.05 us
    pallas_call x1, Pallas kernels, local(): call(krylov, 7, [four, four, four, (1, 128)], [(8, 10) + TILE] * 2 + [(3,...  3.49 us
    pallas_call x1, Pallas kernels, local(): return tuple(call(finish, 5, [four, four])(gram, source, k1, k2, k3))  2.05 us
  transfers between devices with their start and end apart: 4, of which 4 were waited for; matrix products, arithmetic and copies ran while one was open for 0% of the time, Pallas kernels for 0%

profile of v1, /device:TPU:1, one launch (start us, length us, event | category | flops | bytes accessed | tf_op | source)
XLA Modules:
  0.0 75.5 jit_solution(8896411512663838070)
XLA Ops:
  0.6 0.0 copy-start
  0.6 0.9 %copy-done = f32[4,4,8,256]{3,2,1,0:T(8,128)S(1)} copy-done((f32[4,4,8,256]{3,2,1,0:T(8,128)S(1)}, f32[4,4,8,256]{3,2,1,0:T(8,128)}, u32[]{:S(2)}) %copy-start) | copy-done | bytes 131096
  1.5 0.0 copy-start.2
  1.5 0.8 %copy-done.2 = bf16[4,4,8,256]{3,2,1,0:T(8,128)(2,1)S(1)} copy-done((bf16[4,4,8,256]{3,2,1,0:T(8,128)(2,1)S(1)}, bf16[4,4,8,256]{3,2,1,0:T(8,128)(2,1)}, u32[]{:S(2)}) %copy-start.2) | copy-done | bytes 65560
  2.4 0.0 copy-start.3
  2.4 0.8 %copy-done.3 = bf16[3,4,8,256]{3,2,1,0:T(8,128)(2,1)S(1)} copy-done((bf16[3,4,8,256]{3,2,1,0:T(8,128)(2,1)S(1)}, bf16[3,4,8,256]{3,2,1,0:T(8,128)(2,1)}, u32[]{:S(2)}) %copy-start.3) | copy-done | bytes 49176
  3.2 0.0 copy-start.4
  3.2 0.8 %copy-done.4 = s32[4,8,256]{2,1,0:T(8,128)S(1)} copy-done((s32[4,8,256]{2,1,0:T(8,128)S(1)}, s32[4,8,256]{2,1,0:T(8,128)}, u32[]{:S(2)}) %copy-start.4) | copy-done | bytes 32792
  3.9 0.0 copy-start.5
  3.9 0.8 %copy-done.5 = s32[4,8,256]{2,1,0:T(8,128)S(1)} copy-done((s32[4,8,256]{2,1,0:T(8,128)S(1)}, s32[4,8,256]{2,1,0:T(8,128)}, u32[]{:S(2)}) %copy-start.5) | copy-done | bytes 32792
  4.7 0.1 shard_map.68
  4.7 4.0 %collective-permute-start = (f32[19,8,256]{2,1,0:T(8,128)S(1)}, f32[19,8,256]{2,1,0:T(8,128)S(1)}, u32[]{:S(2)}, u32[]{:S(2)}) collective-permute-start(f32[19,8,256]{2,1,0:T(8,128)S(1)} %get-tuple-element.16), channel_id=1, source_target_pairs={{0,1},{1,2},{2,3},{3,4},{4,5},{5,6},{6,7},{7,8},{8,9},{9,10},{10,1... | collective-permute-start | bytes 466952 | tf_op jit(solution)/shard_map/ppermute | solution.py:276
  8.8 1.3 %collective-permute-start.1 = (f32[19,8,256]{2,1,0:T(8,128)S(1)}, f32[19,8,256]{2,1,0:T(8,128)S(1)}, u32[]{:S(2)}, u32[]{:S(2)}) collective-permute-start(f32[19,8,256]{2,1,0:T(8,128)S(1)} %get-tuple-element.17), channel_id=1, source_target_pairs={{1,0},{2,1},{3,2},{4,3},{5,4},{6,5},{7,6},{8,7},{9,8},{10,9},{11,1... | collective-permute-start | bytes 466952 | tf_op jit(solution)/shard_map/ppermute | solution.py:276
  10.1 0.9 %collective-permute-done.from_left = f32[19,8,256]{2,1,0:T(8,128)S(1)} collective-permute-done((f32[19,8,256]{2,1,0:T(8,128)S(1)}, f32[19,8,256]{2,1,0:T(8,128)S(1)}, u32[]{:S(2)}, u32[]{:S(2)}) %collective-permute-start) | collective-permute-done | bytes 155680 | tf_op jit(solution)/shard_map/ppermute | solution.py:276
  10.9 3.8 %collective-permute-done.1.from_right = f32[19,8,256]{2,1,0:T(8,128)S(1)} collective-permute-done((f32[19,8,256]{2,1,0:T(8,128)S(1)}, f32[19,8,256]{2,1,0:T(8,128)S(1)}, u32[]{:S(2)}, u32[]{:S(2)}) %collective-permute-start.1) | collective-permute-done | bytes 155680 | tf_op jit(solution)/shard_map/ppermute | solution.py:276
  14.8 0.1 shard_map.69
  14.9 5.8 %collective-permute-start.2 = (f32[39,8,256]{2,1,0:T(8,128)S(1)}, f32[39,8,256]{2,1,0:T(8,128)S(1)}, u32[]{:S(2)}, u32[]{:S(2)}) collective-permute-start(f32[39,8,256]{2,1,0:T(8,128)S(1)} %get-tuple-element.20), channel_id=1, source_target_pairs={{0,16},{16,32},{32,48},{48,64},{64,80},{80,96},{96,112},{112,128},... | collective-permute-start | bytes 958472 | tf_op jit(solution)/shard_map/ppermute | solution.py:276
  20.7 2.7 %collective-permute-start.3 = (f32[39,8,256]{2,1,0:T(8,128)S(1)}, f32[39,8,256]{2,1,0:T(8,128)S(1)}, u32[]{:S(2)}, u32[]{:S(2)}) collective-permute-start(f32[39,8,256]{2,1,0:T(8,128)S(1)} %get-tuple-element.21), channel_id=1, source_target_pairs={{16,0},{32,16},{48,32},{64,48},{80,64},{96,80},{112,96},{128,112},... | collective-permute-start | bytes 958472 | tf_op jit(solution)/shard_map/ppermute | solution.py:276
  23.4 1.2 %collective-permute-done.2.before = f32[39,8,256]{2,1,0:T(8,128)S(1)} collective-permute-done((f32[39,8,256]{2,1,0:T(8,128)S(1)}, f32[39,8,256]{2,1,0:T(8,128)S(1)}, u32[]{:S(2)}, u32[]{:S(2)}) %collective-permute-start.2) | collective-permute-done | bytes 319520 | tf_op jit(solution)/shard_map/ppermute | solution.py:276
  24.6 4.4 %collective-permute-done.3.after = f32[39,8,256]{2,1,0:T(8,128)S(1)} collective-permute-done((f32[39,8,256]{2,1,0:T(8,128)S(1)}, f32[39,8,256]{2,1,0:T(8,128)S(1)}, u32[]{:S(2)}, u32[]{:S(2)}) %collective-permute-start.3) | collective-permute-done | bytes 319520 | tf_op jit(solution)/shard_map/ppermute | solution.py:276
  29.0 0.0 copy-start.1
  29.0 3.5 %shard_map.70 = (f32[4,4,8,256]{3,2,1,0:T(8,128)S(1)}, f32[4,4,8,256]{3,2,1,0:T(8,128)S(1)}, f32[4,4,8,256]{3,2,1,0:T(8,128)S(1)}, f32[1,128]{1,0:T(1,128)S(1)}) custom-call(f32[4,4,8,256]{3,2,1,0:T(8,128)S(1)} %copy-done, f32[4,4,8,256]{3,2,1,0:T(8,128)S(1)} %get-tuple-element.14.kcell, f32[3,4,8,256]{3,2,1,0:T(8,128)S(1)} %get-tuple-element.15.couple, ...), custom_call_target="tpu_custom_call" | custom-call | tf_op jit(solution)/shard_map/pallas_call | solution.py:290
  32.5 26.8 %all_to_all.10 = f32[32,1,128]{2,1,0:T(1,128)S(1)} all-to-all(f32[32,1,128]{2,1,0:T(1,128)S(1)} %broadcast_in_dim.7), channel_id=1, replica_groups=mesh['gx'=32,'gy'=16] {'gx'}, dimensions={0} | all-to-all | bytes 32768 | tf_op jit(solution)/shard_map/all_to_all | solution.py:298
  59.3 14.2 %all_to_all.11.gram = f32[16,1,128]{2,1,0:T(1,128)S(1)} all-to-all(f32[16,1,128]{2,1,0:T(1,128)S(1)} %broadcast_in_dim.16), channel_id=1, replica_groups=mesh['gx'=32,'gy'=16] {'gy'}, dimensions={0} | all-to-all | bytes 16384 | tf_op jit(solution)/shard_map/all_to_all | solution.py:298
  73.5 0.0 copy-done.1
  73.5 2.1 %shard_map.71 = (f32[4,4,8,256]{3,2,1,0:T(8,128)}, f32[4,4,8,256]{3,2,1,0:T(8,128)}) custom-call(f32[16,1,128]{2,1,0:T(1,128)S(1)} %all_to_all.11.gram, f32[4,4,8,256]{3,2,1,0:T(8,128)S(1)} %copy-done.1, f32[4,4,8,256]{3,2,1,0:T(8,128)S(1)} %get-tuple-element.23.k1, f32[4,4,8,256]{3,2,1,0:T(8,128)S(1)} %get-tuple-element.24.k2, ...), custom_call_target="tpu_custom_call" | custom-call | tf_op jit(solution)/shard_map/pallas_call | solution.py:301
  (3 shorter events, 0.0 us)
Async XLA Ops:
  0.6 0.9 %copy-start = (f32[4,4,8,256]{3,2,1,0:T(8,128)S(1)}, f32[4,4,8,256]{3,2,1,0:T(8,128)}, u32[]{:S(2)}) copy-start(f32[4,4,8,256]{3,2,1,0:T(8,128)} %source.7) | copy-start | bytes 393220
  1.5 0.8 %copy-start.2 = (bf16[4,4,8,256]{3,2,1,0:T(8,128)(2,1)S(1)}, bf16[4,4,8,256]{3,2,1,0:T(8,128)(2,1)}, u32[]{:S(2)}) copy-start(bf16[4,4,8,256]{3,2,1,0:T(8,128)(2,1)} %conduct.1) | copy-start | bytes 196612
  2.4 0.8 %copy-start.3 = (bf16[3,4,8,256]{3,2,1,0:T(8,128)(2,1)S(1)}, bf16[3,4,8,256]{3,2,1,0:T(8,128)(2,1)}, u32[]{:S(2)}) copy-start(bf16[3,4,8,256]{3,2,1,0:T(8,128)(2,1)} %rate.1) | copy-start | bytes 147460
  3.2 0.8 %copy-start.4 = (s32[4,8,256]{2,1,0:T(8,128)S(1)}, s32[4,8,256]{2,1,0:T(8,128)}, u32[]{:S(2)}) copy-start(s32[4,8,256]{2,1,0:T(8,128)} %labels.1) | copy-start | bytes 98308
  3.9 0.8 %copy-start.5 = (s32[4,8,256]{2,1,0:T(8,128)S(1)}, s32[4,8,256]{2,1,0:T(8,128)}, u32[]{:S(2)}) copy-start(s32[4,8,256]{2,1,0:T(8,128)} %mask.1) | copy-start | bytes 98308
  4.7 6.2 %collective-permute-start = (f32[19,8,256]{2,1,0:T(8,128)S(1)}, f32[19,8,256]{2,1,0:T(8,128)S(1)}, u32[]{:S(2)}, u32[]{:S(2)}) collective-permute-start(f32[19,8,256]{2,1,0:T(8,128)S(1)} %get-tuple-element.16), channel_id=1, source_target_pairs={{0,1},{1,2},{2,3},{3,4},{4,5},{5,6},{6,7},{7,8},{8,9},{9,10},{10,1... | collective-permute-start | bytes 466952 | tf_op jit(solution)/shard_map/ppermute | solution.py:276
  8.8 6.0 %collective-permute-start.1 = (f32[19,8,256]{2,1,0:T(8,128)S(1)}, f32[19,8,256]{2,1,0:T(8,128)S(1)}, u32[]{:S(2)}, u32[]{:S(2)}) collective-permute-start(f32[19,8,256]{2,1,0:T(8,128)S(1)} %get-tuple-element.17), channel_id=1, source_target_pairs={{1,0},{2,1},{3,2},{4,3},{5,4},{6,5},{7,6},{8,7},{9,8},{10,9},{11,1... | collective-permute-start | bytes 466952 | tf_op jit(solution)/shard_map/ppermute | solution.py:276
  14.9 9.7 %collective-permute-start.2 = (f32[39,8,256]{2,1,0:T(8,128)S(1)}, f32[39,8,256]{2,1,0:T(8,128)S(1)}, u32[]{:S(2)}, u32[]{:S(2)}) collective-permute-start(f32[39,8,256]{2,1,0:T(8,128)S(1)} %get-tuple-element.20), channel_id=1, source_target_pairs={{0,16},{16,32},{32,48},{48,64},{64,80},{80,96},{96,112},{112,128},... | collective-permute-start | bytes 958472 | tf_op jit(solution)/shard_map/ppermute | solution.py:276
  20.7 8.3 %collective-permute-start.3 = (f32[39,8,256]{2,1,0:T(8,128)S(1)}, f32[39,8,256]{2,1,0:T(8,128)S(1)}, u32[]{:S(2)}, u32[]{:S(2)}) collective-permute-start(f32[39,8,256]{2,1,0:T(8,128)S(1)} %get-tuple-element.21), channel_id=1, source_target_pairs={{16,0},{32,16},{48,32},{64,48},{80,64},{96,80},{112,96},{128,112},... | collective-permute-start | bytes 958472 | tf_op jit(solution)/shard_map/ppermute | solution.py:276
  29.0 44.5 %copy-start.1 = (f32[4,4,8,256]{3,2,1,0:T(8,128)S(1)}, f32[4,4,8,256]{3,2,1,0:T(8,128)}, u32[]{:S(2)}) copy-start(f32[4,4,8,256]{3,2,1,0:T(8,128)} %source.7) | copy-start | bytes 393220

commit v2 on v1

v2 whole, which is shorter than its diff:
```python
import jax
import jax.numpy as jnp
from jax import lax
from jax.experimental import pallas as pl
from jax.experimental.pallas import tpu as pltpu
from jax.sharding import PartitionSpec as P

PHASE = ((1.0, 0.08, 0.08), (1.0, 0.08, 0.08), (0.08, 1.0, 1.0), (0.08, 1.0, 0.08))
SHIFT = (1.0, 0.5, 0.5, 1.0)
WEIGHT = (0.8, 1.0, -1.0, -0.8)
EPS = 1e-12
F32 = jnp.float32
VMEM = pl.BlockSpec(memory_space=pltpu.VMEM)
HBM = pl.BlockSpec(memory_space=pltpu.HBM)
TILE = (8, 256)
Y_TILES = 19
X_TILES = 39
PAIRS = [(i, j) for i in range(4) for j in range(i, 4)]


def rows():
    return lax.broadcasted_iota(jnp.int32, TILE, 0)


def roll(tile, by):
    by = by % 8
    return tile if by == 0 else pltpu.roll(tile, by, 0)


def prepare(source_in, labels_in, mask_in, conduct_in, rate_in,
            source, kcell, couple, to_right, to_left,
            labels, mask, conduct, rate, arrived):
    pairs = ((conduct_in, conduct), (labels_in, labels), (source_in, source), (rate_in, rate), (mask_in, mask))
    copies = [pltpu.make_async_copy(a, b, arrived.at[i]) for i, (a, b) in enumerate(pairs)]
    for c in copies:
        c.start()
    row = rows()

    def faces(f, ref):
        for k in range(2):
            a, b = ref[f % 4, 2 * k], ref[f % 4, 2 * k + 1]
            to_right[2 * f + k] = jnp.where(row >= 5, a, roll(b, -3))
            to_left[2 * f + k] = jnp.where(row < 3, a, roll(b, 3))

    copies[0].wait()
    copies[1].wait()
    for x in range(4):
        phase = labels[x]
        for f in range(4):
            t = PHASE[f]
            base = jnp.where(phase == 0, t[0], jnp.where(phase == 1, t[1], t[2]))
            kcell[f, x] = base * conduct[f, x].astype(F32)
    for f in range(4):
        faces(4 + f, kcell)
    copies[2].wait()
    for f in range(4):
        faces(f, source)
    copies[3].wait()
    copies[4].wait()
    for x in range(4):
        interface = mask[x].astype(F32)
        for f in range(3):
            couple[f, x] = rate[f, x].astype(F32) * interface
    for f in range(3):
        right, left = couple[f, 0], couple[f, 0]
        for x in range(1, 4):
            right = jnp.where(row >= 8 - 2 * x, right, roll(couple[f, x], -2 * x))
            left = jnp.where(row < 2 * x, left, roll(couple[f, x], 2 * x))
        to_right[16 + f] = right
        to_left[16 + f] = left


def widen(source, kcell, couple, from_left, from_right, rim, crim, to_right, to_left):
    row = rows()
    for f in range(8):
        for x in range(4):
            k, b = 2 * f + x // 2, 3 * (x % 2)
            left, right = roll(from_left[k], b), roll(from_right[k], -b)
            rim[f, x] = jnp.where(row < 4, right, left)
    for f in range(3):
        for x in range(4):
            left, right = roll(from_left[16 + f], 2 * x), roll(from_right[16 + f], -2 * x)
            crim[f, x] = jnp.where(row < 4, right, left)
    for out, order in ((to_right, (3, 2, 1)), (to_left, (0, 1, 2))):
        for f in range(8):
            ref = source if f < 4 else kcell
            for d in range(3):
                out[3 * f + d] = ref[f % 4, order[d]]
            out[30 + f] = jnp.where((row == 2) | (row == 3), roll(rim[f, order[1]], 3), rim[f, order[0]])
        for f in range(3):
            for d in range(2):
                out[24 + 2 * f + d] = couple[f, order[d]]
        c = [roll(crim[f, order[0]], 2 * f) for f in range(3)]
        out[38] = jnp.where((row == 0) | (row == 7), c[0], jnp.where(row <= 2, c[1], c[2]))


def krylov(source, kcell, couple, rim, crim, before, after, k1, k2, k3, gram,
           far, cfar, vbody, vedge, dbody, dedge, ubody, uedge):
    row = rows()
    lane = lax.broadcasted_iota(jnp.int32, TILE, 1)
    zero = jnp.zeros(TILE, F32)
    sides = {2: (before, 0), 1: (before, 1), 0: (before, 2), 7: (after, 0), 8: (after, 1), 9: (after, 2)}
    slot = {1: 0, 2: 1, 7: 2, 8: 3}
    for f in range(8):
        for x in (1, 2, 7, 8):
            buf, d = sides[x]
            far[f, slot[x]] = roll(buf[30 + f], -3 * d)
    for f in range(3):
        for buf, k in ((before, 0), (after, 1)):
            cfar[f, k] = roll(buf[38], -2 * f)

    def whole(f, x):
        if 3 <= x <= 6:
            return (source if f < 4 else kcell)[f % 4, x - 3]
        buf, d = sides[x]
        return buf[3 * f + d]

    def border(f, x):
        return rim[f, x - 3] if 3 <= x <= 6 else far[f, slot[x]]

    def couple_body(f, x):
        if 3 <= x <= 6:
            return couple[f, x - 3]
        buf, d = sides[x]
        return buf[24 + 2 * f + d]

    def couple_edge(f, x):
        return crim[f, x - 3] if 3 <= x <= 6 else cfar[f, 0 if x == 2 else 1]

    def along(t, other):
        up = roll(jnp.where(row == 0, other, t), -1)
        down = roll(jnp.where(row == 7, other, t), 1)
        ahead = jnp.where(lane == 255, zero, pltpu.roll(t, 255, 1))
        back = jnp.where(lane == 0, zero, pltpu.roll(t, 1, 1))
        return (up + down) + (ahead + back)

    def mix(v):
        return WEIGHT[0] * (v[0] - v[3]) + (v[1] - v[2])

    def interface(c, v):
        m = mix(v)
        a, b, c = c[0] * m, c[1] * m, c[2] * m
        return [c, -a, a, b]

    for x in range(10):
        for f in range(4):
            ubody[0, f, x] = whole(f, x) * whole(4 + f, x)
            if 1 <= x <= 8:
                uedge[0, f, x] = border(f, x) * border(4 + f, x)

    outs = (None, k1, k2, k3)

    def vector(level, edge, f, x):
        if level == 0:
            return border(f, x) if edge else whole(f, x)
        if edge:
            return vedge[level - 1, f, x]
        return outs[level][f, x - 3] if 3 <= x <= 6 else vbody[level - 1, f, x]

    def step(level, edge, x):
        u, other, diagonal = (uedge, ubody, dedge) if edge else (ubody, uedge, dbody)
        now, later = level % 2, (level + 1) % 2
        v = [vector(level, edge, f, x) for f in range(4)]
        c = interface([(couple_edge if edge else couple_body)(f, x) for f in range(3)], v)
        new = []
        for f in range(4):
            own = border(4 + f, x) if edge else whole(4 + f, x)
            side = border if edge else whole
            if level == 0:
                k = along(own, whole(4 + f, x) if edge else border(4 + f, x))
                k = k + (side(4 + f, x - 1) + side(4 + f, x + 1))
                d = SHIFT[f] + own * k
                diagonal[f, x] = d
            else:
                d = diagonal[f, x]
            s = along(u[now, f, x], other[now, f, x]) + (u[now, f, x - 1] + u[now, f, x + 1])
            t = d * v[f] - own * s + c[f]
            if level < 2:
                u[later, f, x] = own * t
            if edge:
                vedge[level, f, x] = t
            elif 3 <= x <= 6:
                outs[level + 1][f, x - 3] = t
            else:
                vbody[level, f, x] = t
            new.append(t)
        return new

    for level in range(2):
        for x in range(1 + level, 9 - level):
            step(level, False, x)
            if 2 + level <= x <= 7 - level:
                step(level, True, x)
    sums = [zero] * 10
    for x in range(3, 7):
        last = step(2, False, x)
        for f in range(4):
            v = [source[f, x - 3], k1[f, x - 3], k2[f, x - 3], last[f]]
            sums = [s + v[i] * v[j] for s, (i, j) in zip(sums, PAIRS)]
    place = lax.broadcasted_iota(jnp.int32, (1, 128), 1)
    line = jnp.zeros((1, 128), F32)
    for index, s in enumerate(sums):
        whole_sum = jnp.sum(jnp.sum(s, axis=0, keepdims=True), axis=1, keepdims=True)
        line = jnp.where(place == index, whole_sum, line)
    gram[...] = line


def least_squares(columns, beta):
    count = len(columns)
    zero = beta * 0.0
    table = [
        [columns[col][r] if r <= col + 1 else zero for col in range(count)]
        for r in range(count + 1)
    ]
    target = [beta] + [zero] * count
    for col in range(count):
        upper, lower = table[col][col], table[col + 1][col]
        radius = jnp.sqrt(upper * upper + lower * lower)
        cosine, sine = upper / radius, lower / radius
        for other in range(col, count):
            first, second = table[col][other], table[col + 1][other]
            table[col][other] = cosine * first + sine * second
            table[col + 1][other] = -sine * first + cosine * second
        first, second = target[col], target[col + 1]
        target[col] = cosine * first + sine * second
        target[col + 1] = -sine * first + cosine * second
    solved = [zero] * count
    for r in range(count - 1, -1, -1):
        value = target[r]
        for other in range(r + 1, count):
            value = value - table[r][other] * solved[other]
        solved[r] = value / table[r][r]
    return solved


def total(terms):
    out = terms[0]
    for t in terms[1:]:
        out = out + t
    return out


def coefficients(g):
    def dot(u, v):
        return total([total([g[i][j] * v[j] for j in range(len(v))]) * u[i] for i in range(len(u))])

    beta = jnp.sqrt(g[0][0] + EPS)
    basis = [[1.0 / beta]]
    columns = []
    for k in range(3):
        z = [beta * 0.0] + basis[k]
        projections = [dot(basis[i], z) for i in range(k + 1)]
        for i in range(k + 1):
            z = [
                z[j] - projections[i] * basis[i][j] if j < len(basis[i]) else z[j]
                for j in range(k + 2)
            ]
        length = jnp.sqrt(jnp.maximum(dot(z, z), 0.0) + EPS)
        columns.append(projections + [length])
        basis.append([t / length for t in z])
    y = least_squares(columns, beta)
    iterate = [total([y[j] * basis[j][i] for j in range(3) if i < len(basis[j])]) for i in range(3)]
    image = [
        total([columns[col][r] * y[col] for col in range(3) if r <= col + 1]) for r in range(4)
    ]
    image[0] = image[0] - beta
    rest = [-total([image[j] * basis[j][i] for j in range(4) if i < len(basis[j])]) for i in range(4)]
    return iterate, rest


def finish(gram, source, k1, k2, k3, adjoint_out, residual_out, adjoint, residual, left):
    line = gram[0]
    for i in range(1, gram.shape[0]):
        line = line + gram[i]
    g = [[None] * 4 for _ in range(4)]
    for index, (i, j) in enumerate(PAIRS):
        g[i][j] = g[j][i] = line[:, index:index + 1]
    iterate, rest = coefficients(g)
    iterate = [jnp.broadcast_to(t, TILE) for t in iterate]
    rest = [jnp.broadcast_to(t, TILE) for t in rest]
    vectors = (source, k1, k2, k3)
    copies = []
    for f in range(4):
        for x in range(4):
            v = [ref[f, x] for ref in vectors]
            adjoint[f, x] = total([c * t for c, t in zip(iterate, v)])
            residual[f, x] = total([c * t for c, t in zip(rest, v)])
        copies.append(pltpu.make_async_copy(adjoint.at[f], adjoint_out.at[f], left.at[2 * f]))
        copies.append(pltpu.make_async_copy(residual.at[f], residual_out.at[f], left.at[2 * f + 1]))
        for c in copies[-2:]:
            c.start()
    for c in copies:
        c.wait()


def call(kernel, ins, outs, scratch=(), spaces=(VMEM, VMEM)):
    return pl.pallas_call(
        kernel,
        out_shape=[jax.ShapeDtypeStruct(s, F32) for s in outs],
        in_specs=[spaces[0]] * ins,
        out_specs=[spaces[1]] * len(outs),
        scratch_shapes=[s if not isinstance(s, tuple) else pltpu.VMEM(s, F32) for s in scratch],
        compiler_params=pltpu.CompilerParams(vmem_limit_bytes=16 * 2**20),
    )


def swap(to_right, to_left, axis):
    size = lax.axis_size(axis)
    up = [(i, i + 1) for i in range(size - 1)]
    down = [(i + 1, i) for i in range(size - 1)]
    return lax.ppermute(to_right, axis, up), lax.ppermute(to_left, axis, down)


def run_krylov(*args):
    four, wide = (4, 4) + TILE, (4, 10) + TILE
    return call(
        krylov,
        7,
        [four, four, four, (1, 128)],
        [(8, 4) + TILE, (3, 2) + TILE] + [(2, 4, 10) + TILE] * 2 + [wide] * 2 + [(2, 4, 10) + TILE] * 2,
    )(*args)


def run_finish(*args):
    four = (4, 4) + TILE
    own = [four, four, pltpu.SemaphoreType.DMA((8,))]
    return tuple(call(finish, 5, [four, four], own, (VMEM, HBM))(*args))


def local(source, labels, mask, conduct, rate):
    four, three = (4, 4) + TILE, (3, 4) + TILE
    source, kcell, couple, to_right, to_left = call(
        prepare,
        5,
        [four, four, three, (Y_TILES,) + TILE, (Y_TILES,) + TILE],
        [
            pltpu.VMEM((4,) + TILE, jnp.int32),
            pltpu.VMEM((4,) + TILE, jnp.int32),
            pltpu.VMEM(four, jnp.bfloat16),
            pltpu.VMEM(three, jnp.bfloat16),
            pltpu.SemaphoreType.DMA((5,)),
        ],
        (HBM, VMEM),
    )(*[pltpu.with_memory_space_constraint(t, pltpu.HBM) for t in (source, labels, mask, conduct, rate)])
    from_left, from_right = swap(to_right, to_left, "gy")
    rim, crim, to_right, to_left = call(
        widen, 5, [(8, 4) + TILE, three, (X_TILES,) + TILE, (X_TILES,) + TILE]
    )(source, kcell, couple, from_left, from_right)
    before, after = swap(to_right, to_left, "gx")
    k1, k2, k3, gram = run_krylov(source, kcell, couple, rim, crim, before, after)
    for axis in ("gx", "gy"):
        size = lax.axis_size(axis)
        gram = lax.all_to_all(jnp.broadcast_to(gram[None], (size, 1, 128)), axis, 0, 0)
        if axis == "gx":
            gram = jnp.sum(gram, axis=0)
    return run_finish(gram, source, k1, k2, k3)


def solution(mesh):
    return jax.shard_map(
        local,
        mesh=mesh,
        in_specs=(
            P(None, "gx", "gy", None),
            P("gx", "gy", None),
            P("gx", "gy", None),
            P(None, "gx", "gy", None),
            P(None, "gx", "gy", None),
        ),
        out_specs=(P(None, "gx", "gy", None), P(None, "gx", "gy", None)),
        check_vma=False,
    )
```

time: 76 us -> 70.4 us (0.926)
  local copies, waits for them, and re-layouts: 4.08 us -> 0.04 us
  Pallas kernels: 5.67 us -> 4.28 us
    unnamed x12 -> x0, local copies, waits for them, and re-layouts: 4.05 us -> none
    pallas_call x3, Pallas kernels: 5.6 us -> 4.21 us  [the longest x1 2.08 us: run_finish(): return tuple(call(finish, 5, [four, four], own, (VMEM, HBM))(*args))]
where the time goes in v2:
time: 70.4 us; the launch traced here: 70.1 us
  blocking collectives  41 us (58%)
  starting transfers between devices  13.8 us (20%)
  waiting for transfers between devices  10.3 us (15%)
  Pallas kernels  4.28 us (6%)
    all_to_all x2, blocking collectives, local(): lax.all_to_all(jnp.broadcast_to(gram[None], (size, 1, 128)), axis, 0, 0)  41 us
    ppermute x4, starting transfers between devices, swap(): return (lax.ppermute(to_right, axis, up), lax.ppermute(to_left, axis, down))  13.8 us
    ppermute x4, waiting for transfers between devices, swap(): return (lax.ppermute(to_right, axis, up), lax.ppermute(to_left, axis, down))  10.3 us
    pallas_call x1, Pallas kernels, run_finish(): return tuple(call(finish, 5, [four, four], own, (VMEM, HBM))(*args))  2.08 us
  transfers between devices with their start and end apart: 4, of which 4 were waited for; matrix products, arithmetic and copies ran while one was open for 0% of the time, Pallas kernels for 0%

profile of v2, /device:TPU:1, one launch (start us, length us, event | category | flops | bytes accessed | tf_op | source)
XLA Modules:
  0.0 70.1 jit_solution(6938199671076822202)
XLA Ops:
  0.6 1.0 %shard_map.68 = (f32[4,4,8,256]{3,2,1,0:T(8,128)S(1)}, f32[4,4,8,256]{3,2,1,0:T(8,128)S(1)}, f32[3,4,8,256]{3,2,1,0:T(8,128)S(1)}, f32[19,8,256]{2,1,0:T(8,128)S(1)}, f32[19,8,256]{2,1,0:T(8,128)S(1)}) custom-call(f32[4,4,8,256]{3,2,1,0:T(8,128)} %source_in.1, s32[4,8,256]{2,1,0:T(8,128)} %labels_in.1, s32[4,8,256]{2,1,0:T(8,128)} %mask_in.1, ...), custom_call_target="tpu_custom_call" | custom-call | tf_op jit(solution)/shard_map/pallas_call | solution.py:332
  1.7 4.0 %collective-permute-start = (f32[19,8,256]{2,1,0:T(8,128)S(1)}, f32[19,8,256]{2,1,0:T(8,128)S(1)}, u32[]{:S(2)}, u32[]{:S(2)}) collective-permute-start(f32[19,8,256]{2,1,0:T(8,128)S(1)} %get-tuple-element.18), channel_id=1, source_target_pairs={{0,1},{1,2},{2,3},{3,4},{4,5},{5,6},{6,7},{7,8},{8,9},{9,10},{10,1... | collective-permute-start | bytes 466952 | tf_op jit(solution)/shard_map/ppermute | solution.py:311
  5.7 1.3 %collective-permute-start.1 = (f32[19,8,256]{2,1,0:T(8,128)S(1)}, f32[19,8,256]{2,1,0:T(8,128)S(1)}, u32[]{:S(2)}, u32[]{:S(2)}) collective-permute-start(f32[19,8,256]{2,1,0:T(8,128)S(1)} %get-tuple-element.19), channel_id=1, source_target_pairs={{1,0},{2,1},{3,2},{4,3},{5,4},{6,5},{7,6},{8,7},{9,8},{10,9},{11,1... | collective-permute-start | bytes 466952 | tf_op jit(solution)/shard_map/ppermute | solution.py:311
  7.0 0.9 %collective-permute-done.from_left = f32[19,8,256]{2,1,0:T(8,128)S(1)} collective-permute-done((f32[19,8,256]{2,1,0:T(8,128)S(1)}, f32[19,8,256]{2,1,0:T(8,128)S(1)}, u32[]{:S(2)}, u32[]{:S(2)}) %collective-permute-start) | collective-permute-done | bytes 155680 | tf_op jit(solution)/shard_map/ppermute | solution.py:311
  7.9 3.8 %collective-permute-done.1.from_right = f32[19,8,256]{2,1,0:T(8,128)S(1)} collective-permute-done((f32[19,8,256]{2,1,0:T(8,128)S(1)}, f32[19,8,256]{2,1,0:T(8,128)S(1)}, u32[]{:S(2)}, u32[]{:S(2)}) %collective-permute-start.1) | collective-permute-done | bytes 155680 | tf_op jit(solution)/shard_map/ppermute | solution.py:311
  11.7 0.1 shard_map.69
  11.8 5.8 %collective-permute-start.2 = (f32[39,8,256]{2,1,0:T(8,128)S(1)}, f32[39,8,256]{2,1,0:T(8,128)S(1)}, u32[]{:S(2)}, u32[]{:S(2)}) collective-permute-start(f32[39,8,256]{2,1,0:T(8,128)S(1)} %get-tuple-element.22), channel_id=1, source_target_pairs={{0,16},{16,32},{32,48},{48,64},{64,80},{80,96},{96,112},{112,128},... | collective-permute-start | bytes 958472 | tf_op jit(solution)/shard_map/ppermute | solution.py:311
  17.6 2.7 %collective-permute-start.3 = (f32[39,8,256]{2,1,0:T(8,128)S(1)}, f32[39,8,256]{2,1,0:T(8,128)S(1)}, u32[]{:S(2)}, u32[]{:S(2)}) collective-permute-start(f32[39,8,256]{2,1,0:T(8,128)S(1)} %get-tuple-element.23), channel_id=1, source_target_pairs={{16,0},{32,16},{48,32},{64,48},{80,64},{96,80},{112,96},{128,112},... | collective-permute-start | bytes 958472 | tf_op jit(solution)/shard_map/ppermute | solution.py:311
  20.3 1.2 %collective-permute-done.2.before = f32[39,8,256]{2,1,0:T(8,128)S(1)} collective-permute-done((f32[39,8,256]{2,1,0:T(8,128)S(1)}, f32[39,8,256]{2,1,0:T(8,128)S(1)}, u32[]{:S(2)}, u32[]{:S(2)}) %collective-permute-start.2) | collective-permute-done | bytes 319520 | tf_op jit(solution)/shard_map/ppermute | solution.py:311
  21.5 4.4 %collective-permute-done.3.after = f32[39,8,256]{2,1,0:T(8,128)S(1)} collective-permute-done((f32[39,8,256]{2,1,0:T(8,128)S(1)}, f32[39,8,256]{2,1,0:T(8,128)S(1)}, u32[]{:S(2)}, u32[]{:S(2)}) %collective-permute-start.3) | collective-permute-done | bytes 319520 | tf_op jit(solution)/shard_map/ppermute | solution.py:311
  25.9 1.1 %shard_map.70 = (f32[4,4,8,256]{3,2,1,0:T(8,128)S(1)}, f32[4,4,8,256]{3,2,1,0:T(8,128)S(1)}, f32[4,4,8,256]{3,2,1,0:T(8,128)S(1)}, f32[1,128]{1,0:T(1,128)S(1)}) custom-call(f32[4,4,8,256]{3,2,1,0:T(8,128)S(1)} %get-tuple-element.15.source, f32[4,4,8,256]{3,2,1,0:T(8,128)S(1)} %get-tuple-element.16.kcell, f32[3,4,8,256]{3,2,1,0:T(8,128)S(1)} %get-tuple-element.17.couple, ...), custom_call_target="tpu_custom_call" | custom-call | tf_op jit(solution)/shard_map/pallas_call | solution.py:316
  27.0 26.8 %all_to_all.10 = f32[32,1,128]{2,1,0:T(1,128)S(1)} all-to-all(f32[32,1,128]{2,1,0:T(1,128)S(1)} %broadcast_in_dim.7), channel_id=1, replica_groups=mesh['gx'=32,'gy'=16] {'gx'}, dimensions={0} | all-to-all | bytes 32768 | tf_op jit(solution)/shard_map/all_to_all | solution.py:353
  53.8 14.2 %all_to_all.11.gram = f32[16,1,128]{2,1,0:T(1,128)S(1)} all-to-all(f32[16,1,128]{2,1,0:T(1,128)S(1)} %broadcast_in_dim.16), channel_id=1, replica_groups=mesh['gx'=32,'gy'=16] {'gy'}, dimensions={0} | all-to-all | bytes 16384 | tf_op jit(solution)/shard_map/all_to_all | solution.py:353
  68.0 2.1 %shard_map.71 = (f32[4,4,8,256]{3,2,1,0:T(8,128)}, f32[4,4,8,256]{3,2,1,0:T(8,128)}) custom-call(f32[16,1,128]{2,1,0:T(1,128)S(1)} %all_to_all.11.gram, f32[4,4,8,256]{3,2,1,0:T(8,128)S(1)} %get-tuple-element.15.source, f32[4,4,8,256]{3,2,1,0:T(8,128)S(1)} %get-tuple-element.25.k1, f32[4,4,8,256]{3,2,1,0:T(8,128)S(1)} %get-tuple-element.26.k2, ...), custom_call_target="tpu_custom_call" | custom-call | tf_op jit(solution)/shard_map/pallas_call | solution.py:327
  (3 shorter events, 0.1 us)
Async XLA Ops:
  1.7 6.2 %collective-permute-start = (f32[19,8,256]{2,1,0:T(8,128)S(1)}, f32[19,8,256]{2,1,0:T(8,128)S(1)}, u32[]{:S(2)}, u32[]{:S(2)}) collective-permute-start(f32[19,8,256]{2,1,0:T(8,128)S(1)} %get-tuple-element.18), channel_id=1, source_target_pairs={{0,1},{1,2},{2,3},{3,4},{4,5},{5,6},{6,7},{7,8},{8,9},{9,10},{10,1... | collective-permute-start | bytes 466952 | tf_op jit(solution)/shard_map/ppermute | solution.py:311
  5.7 6.0 %collective-permute-start.1 = (f32[19,8,256]{2,1,0:T(8,128)S(1)}, f32[19,8,256]{2,1,0:T(8,128)S(1)}, u32[]{:S(2)}, u32[]{:S(2)}) collective-permute-start(f32[19,8,256]{2,1,0:T(8,128)S(1)} %get-tuple-element.19), channel_id=1, source_target_pairs={{1,0},{2,1},{3,2},{4,3},{5,4},{6,5},{7,6},{8,7},{9,8},{10,9},{11,1... | collective-permute-start | bytes 466952 | tf_op jit(solution)/shard_map/ppermute | solution.py:311
  11.8 9.7 %collective-permute-start.2 = (f32[39,8,256]{2,1,0:T(8,128)S(1)}, f32[39,8,256]{2,1,0:T(8,128)S(1)}, u32[]{:S(2)}, u32[]{:S(2)}) collective-permute-start(f32[39,8,256]{2,1,0:T(8,128)S(1)} %get-tuple-element.22), channel_id=1, source_target_pairs={{0,16},{16,32},{32,48},{48,64},{64,80},{80,96},{96,112},{112,128},... | collective-permute-start | bytes 958472 | tf_op jit(solution)/shard_map/ppermute | solution.py:311
  17.6 8.3 %collective-permute-start.3 = (f32[39,8,256]{2,1,0:T(8,128)S(1)}, f32[39,8,256]{2,1,0:T(8,128)S(1)}, u32[]{:S(2)}, u32[]{:S(2)}) collective-permute-start(f32[39,8,256]{2,1,0:T(8,128)S(1)} %get-tuple-element.23), channel_id=1, source_target_pairs={{16,0},{32,16},{48,32},{64,48},{80,64},{96,80},{112,96},{128,112},... | collective-permute-start | bytes 958472 | tf_op jit(solution)/shard_map/ppermute | solution.py:311

commit v3 on v2

--- a/solution.py
+++ b/solution.py
@@ -14,7 +14,8 @@
 HBM = pl.BlockSpec(memory_space=pltpu.HBM)
 TILE = (8, 256)
 Y_TILES = 19
-X_TILES = 39
+X_TILES = 30
+CORNER_TILES = 9
 PAIRS = [(i, j) for i in range(4) for j in range(i, 4)]
 
 
@@ -70,7 +71,16 @@
         to_left[16 + f] = left
 
 
-def widen(source, kcell, couple, from_left, from_right, rim, crim, to_right, to_left):
+def columns_beside(source, kcell, couple, to_next, to_last):
+    for out, order in ((to_next, (3, 2, 1)), (to_last, (0, 1, 2))):
+        for d in range(3):
+            for f in range(8):
+                out[3 * f + d] = (source if f < 4 else kcell)[f % 4, order[d]]
+            for f in range(3 if d < 2 else 0):
+                out[24 + 2 * f + d] = couple[f, order[d]]
+
+
+def widen(from_left, from_right, rim, crim, to_next, to_last):
     row = rows()
     for f in range(8):
         for x in range(4):
@@ -81,20 +91,15 @@
         for x in range(4):
             left, right = roll(from_left[16 + f], 2 * x), roll(from_right[16 + f], -2 * x)
             crim[f, x] = jnp.where(row < 4, right, left)
-    for out, order in ((to_right, (3, 2, 1)), (to_left, (0, 1, 2))):
+    for out, order in ((to_next, (3, 2)), (to_last, (0, 1))):
         for f in range(8):
-            ref = source if f < 4 else kcell
-            for d in range(3):
-                out[3 * f + d] = ref[f % 4, order[d]]
-            out[30 + f] = jnp.where((row == 2) | (row == 3), roll(rim[f, order[1]], 3), rim[f, order[0]])
-        for f in range(3):
-            for d in range(2):
-                out[24 + 2 * f + d] = couple[f, order[d]]
+            out[f] = jnp.where((row == 2) | (row == 3), roll(rim[f, order[1]], 3), rim[f, order[0]])
         c = [roll(crim[f, order[0]], 2 * f) for f in range(3)]
-        out[38] = jnp.where((row == 0) | (row == 7), c[0], jnp.where(row <= 2, c[1], c[2]))
-
-
-def krylov(source, kcell, couple, rim, crim, before, after, k1, k2, k3, gram,
+        out[8] = jnp.where((row == 0) | (row == 7), c[0], jnp.where(row <= 2, c[1], c[2]))
+
+
+def krylov(source, kcell, couple, rim, crim, before, after, corner_before, corner_after,
+           k1, k2, k3, gram,
            far, cfar, vbody, vedge, dbody, dedge, ubody, uedge):
     row = rows()
     lane = lax.broadcasted_iota(jnp.int32, TILE, 1)
@@ -103,11 +108,11 @@
     slot = {1: 0, 2: 1, 7: 2, 8: 3}
     for f in range(8):
         for x in (1, 2, 7, 8):
-            buf, d = sides[x]
-            far[f, slot[x]] = roll(buf[30 + f], -3 * d)
+            corner = corner_before if x < 3 else corner_after
+            far[f, slot[x]] = roll(corner[f], -3 * sides[x][1])
     for f in range(3):
-        for buf, k in ((before, 0), (after, 1)):
-            cfar[f, k] = roll(buf[38], -2 * f)
+        for corner, k in ((corner_before, 0), (corner_after, 1)):
+            cfar[f, k] = roll(corner[8], -2 * f)
 
     def whole(f, x):
         if 3 <= x <= 6:
@@ -213,11 +218,13 @@
         for r in range(count + 1)
     ]
     target = [beta] + [zero] * count
+    scales = []
     for col in range(count):
         upper, lower = table[col][col], table[col + 1][col]
-        radius = jnp.sqrt(upper * upper + lower * lower)
-        cosine, sine = upper / radius, lower / radius
-        for other in range(col, count):
+        scale = lax.rsqrt(upper * upper + lower * lower)
+        cosine, sine = upper * scale, lower * scale
+        scales.append(scale)
+        for other in range(col + 1, count):
             first, second = table[col][other], table[col + 1][other]
             table[col][other] = cosine * first + sine * second
             table[col + 1][other] = -sine * first + cosine * second
@@ -229,7 +236,7 @@
         value = target[r]
         for other in range(r + 1, count):
             value = value - table[r][other] * solved[other]
-        solved[r] = value / table[r][r]
+        solved[r] = value * scales[r]
     return solved
 
 
@@ -244,8 +251,10 @@
     def dot(u, v):
         return total([total([g[i][j] * v[j] for j in range(len(v))]) * u[i] for i in range(len(u))])
 
-    beta = jnp.sqrt(g[0][0] + EPS)
-    basis = [[1.0 / beta]]
+    square = g[0][0] + EPS
+    inverse = lax.rsqrt(square)
+    beta = square * inverse
+    basis = [[inverse]]
     columns = []
     for k in range(3):
         z = [beta * 0.0] + basis[k]
@@ -255,9 +264,10 @@
                 z[j] - projections[i] * basis[i][j] if j < len(basis[i]) else z[j]
                 for j in range(k + 2)
             ]
-        length = jnp.sqrt(jnp.maximum(dot(z, z), 0.0) + EPS)
-        columns.append(projections + [length])
-        basis.append([t / length for t in z])
+        square = jnp.maximum(dot(z, z), 0.0) + EPS
+        inverse = lax.rsqrt(square)
+        columns.append(projections + [square * inverse])
+        basis.append([t * inverse for t in z])
     y = least_squares(columns, beta)
     iterate = [total([y[j] * basis[j][i] for j in range(3) if i < len(basis[j])]) for i in range(3)]
     image = [
@@ -293,13 +303,14 @@
         c.wait()
 
 
-def call(kernel, ins, outs, scratch=(), spaces=(VMEM, VMEM)):
+def call(kernel, ins, outs, scratch=(), spaces=(VMEM, VMEM), cost=None):
     return pl.pallas_call(
         kernel,
         out_shape=[jax.ShapeDtypeStruct(s, F32) for s in outs],
         in_specs=[spaces[0]] * ins,
         out_specs=[spaces[1]] * len(outs),
         scratch_shapes=[s if not isinstance(s, tuple) else pltpu.VMEM(s, F32) for s in scratch],
+        cost_estimate=cost,
         compiler_params=pltpu.CompilerParams(vmem_limit_bytes=16 * 2**20),
     )
 
@@ -315,7 +326,7 @@
     four, wide = (4, 4) + TILE, (4, 10) + TILE
     return call(
         krylov,
-        7,
+        9,
         [four, four, four, (1, 128)],
         [(8, 4) + TILE, (3, 2) + TILE] + [(2, 4, 10) + TILE] * 2 + [wide] * 2 + [(2, 4, 10) + TILE] * 2,
     )(*args)
@@ -332,7 +343,7 @@
     source, kcell, couple, to_right, to_left = call(
         prepare,
         5,
-        [four, four, three, (Y_TILES,) + TILE, (Y_TILES,) + TILE],
+        [four, four, three] + [(Y_TILES,) + TILE] * 2,
         [
             pltpu.VMEM((4,) + TILE, jnp.int32),
             pltpu.VMEM((4,) + TILE, jnp.int32),
@@ -343,11 +354,19 @@
         (HBM, VMEM),
     )(*[pltpu.with_memory_space_constraint(t, pltpu.HBM) for t in (source, labels, mask, conduct, rate)])
     from_left, from_right = swap(to_right, to_left, "gy")
-    rim, crim, to_right, to_left = call(
-        widen, 5, [(8, 4) + TILE, three, (X_TILES,) + TILE, (X_TILES,) + TILE]
-    )(source, kcell, couple, from_left, from_right)
-    before, after = swap(to_right, to_left, "gx")
-    k1, k2, k3, gram = run_krylov(source, kcell, couple, rim, crim, before, after)
+    to_next, to_last = call(
+        columns_beside, 3, [(X_TILES,) + TILE] * 2,
+        cost=pl.CostEstimate(flops=0, bytes_accessed=10**3, transcendentals=0),
+    )(source, kcell, couple)
+    before, after = swap(to_next, to_last, "gx")
+    rim, crim, to_next, to_last = call(
+        widen, 2, [(8, 4) + TILE, three] + [(CORNER_TILES,) + TILE] * 2,
+        cost=pl.CostEstimate(flops=1000000000, bytes_accessed=10**3, transcendentals=0),
+    )(from_left, from_right)
+    corner_before, corner_after = swap(to_next, to_last, "gx")
+    k1, k2, k3, gram = run_krylov(
+        source, kcell, couple, rim, crim, before, after, corner_before, corner_after
+    )
     for axis in ("gx", "gy"):
         size = lax.axis_size(axis)
         gram = lax.all_to_all(jnp.broadcast_to(gram[None], (size, 1, 128)), axis, 0, 0)

time: 70.4 us -> 68.4 us (0.972)
  waiting for transfers between devices: 10.3 us -> 2.97 us
  starting transfers between devices: 13.8 us -> 18.4 us
    ppermute x4 -> x6, waiting for transfers between devices: 10.3 us -> 2.97 us  [swap(): return (lax.ppermute(to_right, axis, up), lax.ppermute(to_left, axis, down))]
    ppermute x4 -> x6, starting transfers between devices: 13.8 us -> 18.4 us  [swap(): return (lax.ppermute(to_right, axis, up), lax.ppermute(to_left, axis, down))]
    pallas_call x3 -> x4, Pallas kernels: 2.19 us -> 2.23 us  [the longest x1 1.1 us: run_krylov(): call(krylov, 9, [four, four, four, (1, 128)], [(8, 4) + TILE, (3, 2) + TI...]
  transfers between devices with their start and end apart: 4 -> 6, of which waited for: 4 -> 1; matrix products, arithmetic and copies ran while one was open for 0% -> 0% of each run, Pallas kernels for 0% -> 0%
where the time goes in v3:
time: 68.4 us; the launch traced here: 68.1 us
  blocking collectives  41.6 us (61%)
  starting transfers between devices  18.4 us (27%)
  Pallas kernels  4.27 us (6%)
  waiting for transfers between devices  2.97 us (4%)
  between operations  0.74 us (1%)
    all_to_all x2, blocking collectives, local(): lax.all_to_all(jnp.broadcast_to(gram[None], (size, 1, 128)), axis, 0, 0)  41.6 us
    ppermute x6, starting transfers between devices, swap(): return (lax.ppermute(to_right, axis, up), lax.ppermute(to_left, axis, down))  18.4 us
    ppermute x6, waiting for transfers between devices, swap(): return (lax.ppermute(to_right, axis, up), lax.ppermute(to_left, axis, down))  2.97 us
    pallas_call x1, Pallas kernels, run_finish(): return tuple(call(finish, 5, [four, four], own, (VMEM, HBM))(*args))  2.04 us
  transfers between devices with their start and end apart: 6, of which 1 were waited for; matrix products, arithmetic and copies ran while one was open for 0% of the time, Pallas kernels for 0%

profile of v3, /device:TPU:1, one launch (start us, length us, event | category | flops | bytes accessed | tf_op | source)
XLA Modules:
  0.0 68.1 jit_solution(5479881898358218250)
XLA Ops:
  0.6 1.0 %shard_map.68 = (f32[4,4,8,256]{3,2,1,0:T(8,128)S(1)}, f32[4,4,8,256]{3,2,1,0:T(8,128)S(1)}, f32[3,4,8,256]{3,2,1,0:T(8,128)S(1)}, f32[19,8,256]{2,1,0:T(8,128)S(1)}, f32[19,8,256]{2,1,0:T(8,128)S(1)}) custom-call(f32[4,4,8,256]{3,2,1,0:T(8,128)} %source_in.1, s32[4,8,256]{2,1,0:T(8,128)} %labels_in.1, s32[4,8,256]{2,1,0:T(8,128)} %mask_in.1, ...), custom_call_target="tpu_custom_call" | custom-call | tf_op jit(solution)/shard_map/pallas_call | solution.py:343
  1.7 4.0 %collective-permute-start = (f32[19,8,256]{2,1,0:T(8,128)S(1)}, f32[19,8,256]{2,1,0:T(8,128)S(1)}, u32[]{:S(2)}, u32[]{:S(2)}) collective-permute-start(f32[19,8,256]{2,1,0:T(8,128)S(1)} %get-tuple-element.20), channel_id=1, source_target_pairs={{0,1},{1,2},{2,3},{3,4},{4,5},{5,6},{6,7},{7,8},{8,9},{9,10},{10,1... | collective-permute-start | bytes 466952 | tf_op jit(solution)/shard_map/ppermute | solution.py:322
  5.7 1.3 %collective-permute-start.1 = (f32[19,8,256]{2,1,0:T(8,128)S(1)}, f32[19,8,256]{2,1,0:T(8,128)S(1)}, u32[]{:S(2)}, u32[]{:S(2)}) collective-permute-start(f32[19,8,256]{2,1,0:T(8,128)S(1)} %get-tuple-element.21), channel_id=1, source_target_pairs={{1,0},{2,1},{3,2},{4,3},{5,4},{6,5},{7,6},{8,7},{9,8},{10,9},{11,1... | collective-permute-start | bytes 466952 | tf_op jit(solution)/shard_map/ppermute | solution.py:322
  7.1 4.4 %collective-permute-start.2 = (f32[30,8,256]{2,1,0:T(8,128)S(1)}, f32[30,8,256]{2,1,0:T(8,128)S(1)}, u32[]{:S(2)}, u32[]{:S(2)}) collective-permute-start(f32[30,8,256]{2,1,0:T(8,128)S(1)} %get-tuple-element.24), channel_id=1, source_target_pairs={{0,16},{16,32},{32,48},{48,64},{64,80},{80,96},{96,112},{112,128},... | collective-permute-start | bytes 737288 | tf_op jit(solution)/shard_map/ppermute | solution.py:322
  11.5 3.0 %collective-permute-start.3 = (f32[30,8,256]{2,1,0:T(8,128)S(1)}, f32[30,8,256]{2,1,0:T(8,128)S(1)}, u32[]{:S(2)}, u32[]{:S(2)}) collective-permute-start(f32[30,8,256]{2,1,0:T(8,128)S(1)} %get-tuple-element.25), channel_id=1, source_target_pairs={{16,0},{32,16},{48,32},{64,48},{80,64},{96,80},{112,96},{128,112},... | collective-permute-start | bytes 737288 | tf_op jit(solution)/shard_map/ppermute | solution.py:322
  14.4 0.0 collective-permute-done.from_left
  14.4 0.0 collective-permute-done.1.from_right
  14.5 3.0 %collective-permute-start.4 = (f32[9,8,256]{2,1,0:T(8,128)S(1)}, f32[9,8,256]{2,1,0:T(8,128)S(1)}, u32[]{:S(2)}, u32[]{:S(2)}) collective-permute-start(f32[9,8,256]{2,1,0:T(8,128)S(1)} %get-tuple-element.26), channel_id=1, source_target_pairs={{0,16},{16,32},{32,48},{48,64},{64,80},{80,96},{96,112},{112,128},... | collective-permute-start | bytes 221192 | tf_op jit(solution)/shard_map/ppermute | solution.py:322
  17.5 2.7 %collective-permute-start.5 = (f32[9,8,256]{2,1,0:T(8,128)S(1)}, f32[9,8,256]{2,1,0:T(8,128)S(1)}, u32[]{:S(2)}, u32[]{:S(2)}) collective-permute-start(f32[9,8,256]{2,1,0:T(8,128)S(1)} %get-tuple-element.27), channel_id=1, source_target_pairs={{16,0},{32,16},{48,32},{64,48},{80,64},{96,80},{112,96},{128,112},... | collective-permute-start | bytes 221192 | tf_op jit(solution)/shard_map/ppermute | solution.py:322
  20.3 0.0 collective-permute-done.4.corner_before
  20.3 3.0 %collective-permute-done.5.corner_after = f32[9,8,256]{2,1,0:T(8,128)S(1)} collective-permute-done((f32[9,8,256]{2,1,0:T(8,128)S(1)}, f32[9,8,256]{2,1,0:T(8,128)S(1)}, u32[]{:S(2)}, u32[]{:S(2)}) %collective-permute-start.5) | collective-permute-done | bytes 73760 | tf_op jit(solution)/shard_map/ppermute | solution.py:322
  23.2 0.0 collective-permute-done.2.before
  23.2 0.0 collective-permute-done.3.after
  23.2 1.1 %shard_map.71 = (f32[4,4,8,256]{3,2,1,0:T(8,128)S(1)}, f32[4,4,8,256]{3,2,1,0:T(8,128)S(1)}, f32[4,4,8,256]{3,2,1,0:T(8,128)S(1)}, f32[1,128]{1,0:T(1,128)S(1)}) custom-call(f32[4,4,8,256]{3,2,1,0:T(8,128)S(1)} %get-tuple-element.17.source, f32[4,4,8,256]{3,2,1,0:T(8,128)S(1)} %get-tuple-element.18.kcell, f32[3,4,8,256]{3,2,1,0:T(8,128)S(1)} %get-tuple-element.19.couple, ...), custom_call_target="tpu_custom_call" | custom-call | tf_op jit(solution)/shard_map/pallas_call | solution.py:327
  24.4 27.6 %all_to_all.10 = f32[32,1,128]{2,1,0:T(1,128)S(1)} all-to-all(f32[32,1,128]{2,1,0:T(1,128)S(1)} %broadcast_in_dim.7), channel_id=1, replica_groups=mesh['gx'=32,'gy'=16] {'gx'}, dimensions={0} | all-to-all | bytes 32768 | tf_op jit(solution)/shard_map/all_to_all | solution.py:372
  52.0 14.0 %all_to_all.11.gram = f32[16,1,128]{2,1,0:T(1,128)S(1)} all-to-all(f32[16,1,128]{2,1,0:T(1,128)S(1)} %broadcast_in_dim.16), channel_id=1, replica_groups=mesh['gx'=32,'gy'=16] {'gy'}, dimensions={0} | all-to-all | bytes 16384 | tf_op jit(solution)/shard_map/all_to_all | solution.py:372
  66.0 2.0 %shard_map.72 = (f32[4,4,8,256]{3,2,1,0:T(8,128)}, f32[4,4,8,256]{3,2,1,0:T(8,128)}) custom-call(f32[16,1,128]{2,1,0:T(1,128)S(1)} %all_to_all.11.gram, f32[4,4,8,256]{3,2,1,0:T(8,128)S(1)} %get-tuple-element.17.source, f32[4,4,8,256]{3,2,1,0:T(8,128)S(1)} %get-tuple-element.29.k1, f32[4,4,8,256]{3,2,1,0:T(8,128)S(1)} %get-tuple-element.30.k2, ...), custom_call_target="tpu_custom_call" | custom-call | tf_op jit(solution)/shard_map/pallas_call | solution.py:338
  (5 shorter events, 0.1 us)
Async XLA Ops:
  1.7 12.8 %collective-permute-start = (f32[19,8,256]{2,1,0:T(8,128)S(1)}, f32[19,8,256]{2,1,0:T(8,128)S(1)}, u32[]{:S(2)}, u32[]{:S(2)}) collective-permute-start(f32[19,8,256]{2,1,0:T(8,128)S(1)} %get-tuple-element.20), channel_id=1, source_target_pairs={{0,1},{1,2},{2,3},{3,4},{4,5},{5,6},{6,7},{7,8},{8,9},{9,10},{10,1... | collective-permute-start | bytes 466952 | tf_op jit(solution)/shard_map/ppermute | solution.py:322
  5.7 8.7 %collective-permute-start.1 = (f32[19,8,256]{2,1,0:T(8,128)S(1)}, f32[19,8,256]{2,1,0:T(8,128)S(1)}, u32[]{:S(2)}, u32[]{:S(2)}) collective-permute-start(f32[19,8,256]{2,1,0:T(8,128)S(1)} %get-tuple-element.21), channel_id=1, source_target_pairs={{1,0},{2,1},{3,2},{4,3},{5,4},{6,5},{7,6},{8,7},{9,8},{10,9},{11,1... | collective-permute-start | bytes 466952 | tf_op jit(solution)/shard_map/ppermute | solution.py:322
  7.1 16.2 %collective-permute-start.2 = (f32[30,8,256]{2,1,0:T(8,128)S(1)}, f32[30,8,256]{2,1,0:T(8,128)S(1)}, u32[]{:S(2)}, u32[]{:S(2)}) collective-permute-start(f32[30,8,256]{2,1,0:T(8,128)S(1)} %get-tuple-element.24), channel_id=1, source_target_pairs={{0,16},{16,32},{32,48},{48,64},{64,80},{80,96},{96,112},{112,128},... | collective-permute-start | bytes 737288 | tf_op jit(solution)/shard_map/ppermute | solution.py:322
  11.5 11.8 %collective-permute-start.3 = (f32[30,8,256]{2,1,0:T(8,128)S(1)}, f32[30,8,256]{2,1,0:T(8,128)S(1)}, u32[]{:S(2)}, u32[]{:S(2)}) collective-permute-start(f32[30,8,256]{2,1,0:T(8,128)S(1)} %get-tuple-element.25), channel_id=1, source_target_pairs={{16,0},{32,16},{48,32},{64,48},{80,64},{96,80},{112,96},{128,112},... | collective-permute-start | bytes 737288 | tf_op jit(solution)/shard_map/ppermute | solution.py:322
  14.5 5.7 %collective-permute-start.4 = (f32[9,8,256]{2,1,0:T(8,128)S(1)}, f32[9,8,256]{2,1,0:T(8,128)S(1)}, u32[]{:S(2)}, u32[]{:S(2)}) collective-permute-start(f32[9,8,256]{2,1,0:T(8,128)S(1)} %get-tuple-element.26), channel_id=1, source_target_pairs={{0,16},{16,32},{32,48},{48,64},{64,80},{80,96},{96,112},{112,128},... | collective-permute-start | bytes 221192 | tf_op jit(solution)/shard_map/ppermute | solution.py:322
  17.5 5.7 %collective-permute-start.5 = (f32[9,8,256]{2,1,0:T(8,128)S(1)}, f32[9,8,256]{2,1,0:T(8,128)S(1)}, u32[]{:S(2)}, u32[]{:S(2)}) collective-permute-start(f32[9,8,256]{2,1,0:T(8,128)S(1)} %get-tuple-element.27), channel_id=1, source_target_pairs={{16,0},{32,16},{48,32},{64,48},{80,64},{96,80},{112,96},{128,112},... | collective-permute-start | bytes 221192 | tf_op jit(solution)/shard_map/ppermute | solution.py:322

commit v4 on v3

--- a/solution.py
+++ b/solution.py
@@ -71,8 +71,14 @@
         to_left[16 + f] = left
 
 
-def columns_beside(source, kcell, couple, to_next, to_last):
-    for out, order in ((to_next, (3, 2, 1)), (to_last, (0, 1, 2))):
+def columns_from_partner():
+    odd = lax.axis_index("gx") % 2
+    return [k + (1 - odd) * (3 - 2 * k) for k in range(4)]
+
+
+def columns_beside(source, kcell, couple, to_partner, to_other):
+    own = columns_from_partner()
+    for out, order in ((to_partner, own[:3]), (to_other, own[:0:-1])):
         for d in range(3):
             for f in range(8):
                 out[3 * f + d] = (source if f < 4 else kcell)[f % 4, order[d]]
@@ -80,7 +86,7 @@
                 out[24 + 2 * f + d] = couple[f, order[d]]
 
 
-def widen(from_left, from_right, rim, crim, to_next, to_last):
+def widen(from_left, from_right, rim, crim, to_partner, to_other):
     row = rows()
     for f in range(8):
         for x in range(4):
@@ -91,46 +97,48 @@
         for x in range(4):
             left, right = roll(from_left[16 + f], 2 * x), roll(from_right[16 + f], -2 * x)
             crim[f, x] = jnp.where(row < 4, right, left)
-    for out, order in ((to_next, (3, 2)), (to_last, (0, 1))):
+    own = columns_from_partner()
+    for out, order in ((to_partner, own[:2]), (to_other, own[:1:-1])):
         for f in range(8):
             out[f] = jnp.where((row == 2) | (row == 3), roll(rim[f, order[1]], 3), rim[f, order[0]])
         c = [roll(crim[f, order[0]], 2 * f) for f in range(3)]
         out[8] = jnp.where((row == 0) | (row == 7), c[0], jnp.where(row <= 2, c[1], c[2]))
 
 
-def krylov(source, kcell, couple, rim, crim, before, after, corner_before, corner_after,
+def krylov(source, kcell, couple, rim, crim, far, near, far_corner, near_corner,
            k1, k2, k3, gram,
-           far, cfar, vbody, vedge, dbody, dedge, ubody, uedge):
+           border_x, border_c, vbody, vedge, dbody, dedge, ubody, uedge):
     row = rows()
     lane = lax.broadcasted_iota(jnp.int32, TILE, 1)
     zero = jnp.zeros(TILE, F32)
-    sides = {2: (before, 0), 1: (before, 1), 0: (before, 2), 7: (after, 0), 8: (after, 1), 9: (after, 2)}
+    own = columns_from_partner()
+    sides = {2: (near, 0), 1: (near, 1), 0: (near, 2), 7: (far, 0), 8: (far, 1), 9: (far, 2)}
     slot = {1: 0, 2: 1, 7: 2, 8: 3}
     for f in range(8):
         for x in (1, 2, 7, 8):
-            corner = corner_before if x < 3 else corner_after
-            far[f, slot[x]] = roll(corner[f], -3 * sides[x][1])
+            corner = near_corner if x < 3 else far_corner
+            border_x[f, slot[x]] = roll(corner[f], -3 * sides[x][1])
     for f in range(3):
-        for corner, k in ((corner_before, 0), (corner_after, 1)):
-            cfar[f, k] = roll(corner[8], -2 * f)
+        for corner, k in ((near_corner, 0), (far_corner, 1)):
+            border_c[f, k] = roll(corner[8], -2 * f)
 
     def whole(f, x):
         if 3 <= x <= 6:
-            return (source if f < 4 else kcell)[f % 4, x - 3]
+            return (source if f < 4 else kcell)[f % 4, own[x - 3]]
         buf, d = sides[x]
         return buf[3 * f + d]
 
     def border(f, x):
-        return rim[f, x - 3] if 3 <= x <= 6 else far[f, slot[x]]
+        return rim[f, own[x - 3]] if 3 <= x <= 6 else border_x[f, slot[x]]
 
     def couple_body(f, x):
         if 3 <= x <= 6:
-            return couple[f, x - 3]
+            return couple[f, own[x - 3]]
         buf, d = sides[x]
         return buf[24 + 2 * f + d]
 
     def couple_edge(f, x):
-        return crim[f, x - 3] if 3 <= x <= 6 else cfar[f, 0 if x == 2 else 1]
+        return crim[f, own[x - 3]] if 3 <= x <= 6 else border_c[f, 0 if x == 2 else 1]
 
     def along(t, other):
         up = roll(jnp.where(row == 0, other, t), -1)
@@ -160,7 +168,7 @@
             return border(f, x) if edge else whole(f, x)
         if edge:
             return vedge[level - 1, f, x]
-        return outs[level][f, x - 3] if 3 <= x <= 6 else vbody[level - 1, f, x]
+        return outs[level][f, own[x - 3]] if 3 <= x <= 6 else vbody[level - 1, f, x]
 
     def step(level, edge, x):
         u, other, diagonal = (uedge, ubody, dedge) if edge else (ubody, uedge, dbody)
@@ -169,23 +177,23 @@
         c = interface([(couple_edge if edge else couple_body)(f, x) for f in range(3)], v)
         new = []
         for f in range(4):
-            own = border(4 + f, x) if edge else whole(4 + f, x)
+            here = border(4 + f, x) if edge else whole(4 + f, x)
             side = border if edge else whole
             if level == 0:
-                k = along(own, whole(4 + f, x) if edge else border(4 + f, x))
+                k = along(here, whole(4 + f, x) if edge else border(4 + f, x))
                 k = k + (side(4 + f, x - 1) + side(4 + f, x + 1))
-                d = SHIFT[f] + own * k
+                d = SHIFT[f] + here * k
                 diagonal[f, x] = d
             else:
                 d = diagonal[f, x]
             s = along(u[now, f, x], other[now, f, x]) + (u[now, f, x - 1] + u[now, f, x + 1])
-            t = d * v[f] - own * s + c[f]
+            t = d * v[f] - here * s + c[f]
             if level < 2:
-                u[later, f, x] = own * t
+                u[later, f, x] = here * t
             if edge:
                 vedge[level, f, x] = t
             elif 3 <= x <= 6:
-                outs[level + 1][f, x - 3] = t
+                outs[level + 1][f, own[x - 3]] = t
             else:
                 vbody[level, f, x] = t
             new.append(t)
@@ -200,7 +208,7 @@
     for x in range(3, 7):
         last = step(2, False, x)
         for f in range(4):
-            v = [source[f, x - 3], k1[f, x - 3], k2[f, x - 3], last[f]]
+            v = [source[f, own[x - 3]], k1[f, own[x - 3]], k2[f, own[x - 3]], last[f]]
             sums = [s + v[i] * v[j] for s, (i, j) in zip(sums, PAIRS)]
     place = lax.broadcasted_iota(jnp.int32, (1, 128), 1)
     line = jnp.zeros((1, 128), F32)
@@ -322,6 +330,13 @@
     return lax.ppermute(to_right, axis, up), lax.ppermute(to_left, axis, down)
 
 
+def exchange(to_partner, to_other):
+    size = lax.axis_size("gx")
+    chip = [(i, i ^ 1) for i in range(size)]
+    across = [(i, ((i + 1) ^ 1) - 1) for i in range(1, size - 1)]
+    return lax.ppermute(to_other, "gx", across), lax.ppermute(to_partner, "gx", chip)
+
+
 def run_krylov(*args):
     four, wide = (4, 4) + TILE, (4, 10) + TILE
     return call(
@@ -354,18 +369,18 @@
         (HBM, VMEM),
     )(*[pltpu.with_memory_space_constraint(t, pltpu.HBM) for t in (source, labels, mask, conduct, rate)])
     from_left, from_right = swap(to_right, to_left, "gy")
-    to_next, to_last = call(
+    to_partner, to_other = call(
         columns_beside, 3, [(X_TILES,) + TILE] * 2,
         cost=pl.CostEstimate(flops=0, bytes_accessed=10**3, transcendentals=0),
     )(source, kcell, couple)
-    before, after = swap(to_next, to_last, "gx")
-    rim, crim, to_next, to_last = call(
+    far, near = exchange(to_partner, to_other)
+    rim, crim, to_partner, to_other = call(
         widen, 2, [(8, 4) + TILE, three] + [(CORNER_TILES,) + TILE] * 2,
         cost=pl.CostEstimate(flops=1000000000, bytes_accessed=10**3, transcendentals=0),
     )(from_left, from_right)
-    corner_before, corner_after = swap(to_next, to_last, "gx")
+    far_corner, near_corner = exchange(to_partner, to_other)
     k1, k2, k3, gram = run_krylov(
-        source, kcell, couple, rim, crim, before, after, corner_before, corner_after
+        source, kcell, couple, rim, crim, far, near, far_corner, near_corner
     )
     for axis in ("gx", "gy"):
         size = lax.axis_size(axis)

time: 68.4 us -> 65.6 us (0.959)
  waiting for transfers between devices: 2.97 us -> 1.08 us
    ppermute x6 -> x2, starting transfers between devices: 18.4 us -> 5.33 us  [swap(): return (lax.ppermute(to_right, axis, up), lax.ppermute(to_left, axis, down))]
    ppermute x0 -> x4, starting transfers between devices: none -> 12.4 us  [the longest x2 8.03 us: exchange(): lax.ppermute(to_other, 'gx', across)]
    ppermute x6 -> x2, waiting for transfers between devices: 2.97 us -> 0.01 us  [swap(): return (lax.ppermute(to_right, axis, up), lax.ppermute(to_left, axis, down))]
    ppermute x0 -> x4, waiting for transfers between devices: none -> 1.08 us  [the longest x2 1.07 us: exchange(): lax.ppermute(to_partner, 'gx', chip)]
where the time goes in v4:
time: 65.6 us; the launch traced here: 65.3 us
  blocking collectives  41.3 us (63%)
  starting transfers between devices  17.8 us (27%)
  Pallas kernels  4.31 us (7%)
  waiting for transfers between devices  1.08 us (2%)
  between operations  0.74 us (1%)
    all_to_all x2, blocking collectives, local(): lax.all_to_all(jnp.broadcast_to(gram[None], (size, 1, 128)), axis, 0, 0)  41.3 us
    ppermute x2, starting transfers between devices, exchange(): lax.ppermute(to_other, 'gx', across)  8.03 us
    ppermute x2, starting transfers between devices, swap(): return (lax.ppermute(to_right, axis, up), lax.ppermute(to_left, axis, down))  5.33 us
    ppermute x2, starting transfers between devices, exchange(): lax.ppermute(to_partner, 'gx', chip)  4.41 us
    pallas_call x1, Pallas kernels, run_finish(): return tuple(call(finish, 5, [four, four], own, (VMEM, HBM))(*args))  2.04 us
  transfers between devices with their start and end apart: 6, of which 1 were waited for; matrix products, arithmetic and copies ran while one was open for 0% of the time, Pallas kernels for 0%

profile of v4, /device:TPU:1, one launch (start us, length us, event | category | flops | bytes accessed | tf_op | source)
XLA Modules:
  0.0 65.3 jit_solution(15195575195002406055)
XLA Ops:
  0.6 1.0 %shard_map.68 = (f32[4,4,8,256]{3,2,1,0:T(8,128)S(1)}, f32[4,4,8,256]{3,2,1,0:T(8,128)S(1)}, f32[3,4,8,256]{3,2,1,0:T(8,128)S(1)}, f32[19,8,256]{2,1,0:T(8,128)S(1)}, f32[19,8,256]{2,1,0:T(8,128)S(1)}) custom-call(f32[4,4,8,256]{3,2,1,0:T(8,128)} %source_in.1, s32[4,8,256]{2,1,0:T(8,128)} %labels_in.1, s32[4,8,256]{2,1,0:T(8,128)} %mask_in.1, ...), custom_call_target="tpu_custom_call" | custom-call | tf_op jit(solution)/shard_map/pallas_call | solution.py:358
  1.7 4.0 %collective-permute-start = (f32[19,8,256]{2,1,0:T(8,128)S(1)}, f32[19,8,256]{2,1,0:T(8,128)S(1)}, u32[]{:S(2)}, u32[]{:S(2)}) collective-permute-start(f32[19,8,256]{2,1,0:T(8,128)S(1)} %get-tuple-element.20), channel_id=1, source_target_pairs={{0,1},{1,2},{2,3},{3,4},{4,5},{5,6},{6,7},{7,8},{8,9},{9,10},{10,1... | collective-permute-start | bytes 466952 | tf_op jit(solution)/shard_map/ppermute | solution.py:330
  5.7 1.3 %collective-permute-start.1 = (f32[19,8,256]{2,1,0:T(8,128)S(1)}, f32[19,8,256]{2,1,0:T(8,128)S(1)}, u32[]{:S(2)}, u32[]{:S(2)}) collective-permute-start(f32[19,8,256]{2,1,0:T(8,128)S(1)} %get-tuple-element.21), channel_id=1, source_target_pairs={{1,0},{2,1},{3,2},{4,3},{5,4},{6,5},{7,6},{8,7},{9,8},{10,9},{11,1... | collective-permute-start | bytes 466952 | tf_op jit(solution)/shard_map/ppermute | solution.py:330
  7.1 4.4 %collective-permute-start.2 = (f32[30,8,256]{2,1,0:T(8,128)S(1)}, f32[30,8,256]{2,1,0:T(8,128)S(1)}, u32[]{:S(2)}, u32[]{:S(2)}) collective-permute-start(f32[30,8,256]{2,1,0:T(8,128)S(1)} %get-tuple-element.24), channel_id=1, source_target_pairs={{16,32},{32,16},{48,64},{64,48},{80,96},{96,80},{112,128},{128,112... | collective-permute-start | bytes 737288 | tf_op jit(solution)/shard_map/ppermute | solution.py:337
  11.5 2.3 %collective-permute-start.3 = (f32[30,8,256]{2,1,0:T(8,128)S(1)}, f32[30,8,256]{2,1,0:T(8,128)S(1)}, u32[]{:S(2)}, u32[]{:S(2)}) collective-permute-start(f32[30,8,256]{2,1,0:T(8,128)S(1)} %get-tuple-element.25), channel_id=1, source_target_pairs={{0,16},{16,0},{32,48},{48,32},{64,80},{80,64},{96,112},{112,96},{1... | collective-permute-start | bytes 737288 | tf_op jit(solution)/shard_map/ppermute | solution.py:337
  13.8 0.0 collective-permute-done.from_left
  13.8 0.0 collective-permute-done.1.from_right
  13.9 3.6 %collective-permute-start.4 = (f32[9,8,256]{2,1,0:T(8,128)S(1)}, f32[9,8,256]{2,1,0:T(8,128)S(1)}, u32[]{:S(2)}, u32[]{:S(2)}) collective-permute-start(f32[9,8,256]{2,1,0:T(8,128)S(1)} %get-tuple-element.26), channel_id=1, source_target_pairs={{16,32},{32,16},{48,64},{64,48},{80,96},{96,80},{112,128},{128,112... | collective-permute-start | bytes 221192 | tf_op jit(solution)/shard_map/ppermute | solution.py:337
  17.5 2.1 %collective-permute-start.5 = (f32[9,8,256]{2,1,0:T(8,128)S(1)}, f32[9,8,256]{2,1,0:T(8,128)S(1)}, u32[]{:S(2)}, u32[]{:S(2)}) collective-permute-start(f32[9,8,256]{2,1,0:T(8,128)S(1)} %get-tuple-element.27), channel_id=1, source_target_pairs={{0,16},{16,0},{32,48},{48,32},{64,80},{80,64},{96,112},{112,96},{1... | collective-permute-start | bytes 221192 | tf_op jit(solution)/shard_map/ppermute | solution.py:337
  19.6 0.0 collective-permute-done.4.far_corner
  19.6 1.1 %collective-permute-done.5.near_corner = f32[9,8,256]{2,1,0:T(8,128)S(1)} collective-permute-done((f32[9,8,256]{2,1,0:T(8,128)S(1)}, f32[9,8,256]{2,1,0:T(8,128)S(1)}, u32[]{:S(2)}, u32[]{:S(2)}) %collective-permute-start.5) | collective-permute-done | bytes 73760 | tf_op jit(solution)/shard_map/ppermute | solution.py:337
  20.7 0.0 collective-permute-done.2.far
  20.7 0.0 collective-permute-done.3.near
  20.7 1.1 %shard_map.71 = (f32[4,4,8,256]{3,2,1,0:T(8,128)S(1)}, f32[4,4,8,256]{3,2,1,0:T(8,128)S(1)}, f32[4,4,8,256]{3,2,1,0:T(8,128)S(1)}, f32[1,128]{1,0:T(1,128)S(1)}) custom-call(f32[4,4,8,256]{3,2,1,0:T(8,128)S(1)} %get-tuple-element.17.source, f32[4,4,8,256]{3,2,1,0:T(8,128)S(1)} %get-tuple-element.18.kcell, f32[3,4,8,256]{3,2,1,0:T(8,128)S(1)} %get-tuple-element.19.couple, ...), custom_call_target="tpu_custom_call" | custom-call | tf_op jit(solution)/shard_map/pallas_call | solution.py:342
  21.9 27.1 %all_to_all.10 = f32[32,1,128]{2,1,0:T(1,128)S(1)} all-to-all(f32[32,1,128]{2,1,0:T(1,128)S(1)} %broadcast_in_dim.7), channel_id=1, replica_groups=mesh['gx'=32,'gy'=16] {'gx'}, dimensions={0} | all-to-all | bytes 32768 | tf_op jit(solution)/shard_map/all_to_all | solution.py:387
  49.0 14.2 %all_to_all.11.gram = f32[16,1,128]{2,1,0:T(1,128)S(1)} all-to-all(f32[16,1,128]{2,1,0:T(1,128)S(1)} %broadcast_in_dim.16), channel_id=1, replica_groups=mesh['gx'=32,'gy'=16] {'gy'}, dimensions={0} | all-to-all | bytes 16384 | tf_op jit(solution)/shard_map/all_to_all | solution.py:387
  63.2 2.0 %shard_map.72 = (f32[4,4,8,256]{3,2,1,0:T(8,128)}, f32[4,4,8,256]{3,2,1,0:T(8,128)}) custom-call(f32[16,1,128]{2,1,0:T(1,128)S(1)} %all_to_all.11.gram, f32[4,4,8,256]{3,2,1,0:T(8,128)S(1)} %get-tuple-element.17.source, f32[4,4,8,256]{3,2,1,0:T(8,128)S(1)} %get-tuple-element.29.k1, f32[4,4,8,256]{3,2,1,0:T(8,128)S(1)} %get-tuple-element.30.k2, ...), custom_call_target="tpu_custom_call" | custom-call | tf_op jit(solution)/shard_map/pallas_call | solution.py:353
  (5 shorter events, 0.2 us)
Async XLA Ops:
  1.7 12.1 %collective-permute-start = (f32[19,8,256]{2,1,0:T(8,128)S(1)}, f32[19,8,256]{2,1,0:T(8,128)S(1)}, u32[]{:S(2)}, u32[]{:S(2)}) collective-permute-start(f32[19,8,256]{2,1,0:T(8,128)S(1)} %get-tuple-element.20), channel_id=1, source_target_pairs={{0,1},{1,2},{2,3},{3,4},{4,5},{5,6},{6,7},{7,8},{8,9},{9,10},{10,1... | collective-permute-start | bytes 466952 | tf_op jit(solution)/shard_map/ppermute | solution.py:330
  5.7 8.1 %collective-permute-start.1 = (f32[19,8,256]{2,1,0:T(8,128)S(1)}, f32[19,8,256]{2,1,0:T(8,128)S(1)}, u32[]{:S(2)}, u32[]{:S(2)}) collective-permute-start(f32[19,8,256]{2,1,0:T(8,128)S(1)} %get-tuple-element.21), channel_id=1, source_target_pairs={{1,0},{2,1},{3,2},{4,3},{5,4},{6,5},{7,6},{8,7},{9,8},{10,9},{11,1... | collective-permute-start | bytes 466952 | tf_op jit(solution)/shard_map/ppermute | solution.py:330
  7.1 13.6 %collective-permute-start.2 = (f32[30,8,256]{2,1,0:T(8,128)S(1)}, f32[30,8,256]{2,1,0:T(8,128)S(1)}, u32[]{:S(2)}, u32[]{:S(2)}) collective-permute-start(f32[30,8,256]{2,1,0:T(8,128)S(1)} %get-tuple-element.24), channel_id=1, source_target_pairs={{16,32},{32,16},{48,64},{64,48},{80,96},{96,80},{112,128},{128,112... | collective-permute-start | bytes 737288 | tf_op jit(solution)/shard_map/ppermute | solution.py:337
  11.5 9.2 %collective-permute-start.3 = (f32[30,8,256]{2,1,0:T(8,128)S(1)}, f32[30,8,256]{2,1,0:T(8,128)S(1)}, u32[]{:S(2)}, u32[]{:S(2)}) collective-permute-start(f32[30,8,256]{2,1,0:T(8,128)S(1)} %get-tuple-element.25), channel_id=1, source_target_pairs={{0,16},{16,0},{32,48},{48,32},{64,80},{80,64},{96,112},{112,96},{1... | collective-permute-start | bytes 737288 | tf_op jit(solution)/shard_map/ppermute | solution.py:337
  13.9 5.7 %collective-permute-start.4 = (f32[9,8,256]{2,1,0:T(8,128)S(1)}, f32[9,8,256]{2,1,0:T(8,128)S(1)}, u32[]{:S(2)}, u32[]{:S(2)}) collective-permute-start(f32[9,8,256]{2,1,0:T(8,128)S(1)} %get-tuple-element.26), channel_id=1, source_target_pairs={{16,32},{32,16},{48,64},{64,48},{80,96},{96,80},{112,128},{128,112... | collective-permute-start | bytes 221192 | tf_op jit(solution)/shard_map/ppermute | solution.py:337
  17.5 3.2 %collective-permute-start.5 = (f32[9,8,256]{2,1,0:T(8,128)S(1)}, f32[9,8,256]{2,1,0:T(8,128)S(1)}, u32[]{:S(2)}, u32[]{:S(2)}) collective-permute-start(f32[9,8,256]{2,1,0:T(8,128)S(1)} %get-tuple-element.27), channel_id=1, source_target_pairs={{0,16},{16,0},{32,48},{48,32},{64,80},{80,64},{96,112},{112,96},{1... | collective-permute-start | bytes 221192 | tf_op jit(solution)/shard_map/ppermute | solution.py:337

commit v5 on v4

--- a/solution.py
+++ b/solution.py
@@ -292,10 +292,10 @@
         line = line + gram[i]
     g = [[None] * 4 for _ in range(4)]
     for index, (i, j) in enumerate(PAIRS):
-        g[i][j] = g[j][i] = line[:, index:index + 1]
+        g[i][j] = g[j][i] = jnp.broadcast_to(line[:, index:index + 1], (8, 128))
     iterate, rest = coefficients(g)
-    iterate = [jnp.broadcast_to(t, TILE) for t in iterate]
-    rest = [jnp.broadcast_to(t, TILE) for t in rest]
+    iterate = [jnp.concatenate([t, t], axis=1) for t in iterate]
+    rest = [jnp.concatenate([t, t], axis=1) for t in rest]
     vectors = (source, k1, k2, k3)
     copies = []
     for f in range(4):

time: 65.6 us -> 64.5 us (0.983)
  Pallas kernels: 4.31 us -> 3.22 us
    pallas_call x1, Pallas kernels: 2.04 us -> 0.95 us  [run_finish(): return tuple(call(finish, 5, [four, four], own, (VMEM, HBM))(*args))]
where the time goes in v5:
time: 64.5 us; the launch traced here: 64.2 us
  blocking collectives  41.3 us (64%)
  starting transfers between devices  17.8 us (28%)
  Pallas kernels  3.22 us (5%)
  waiting for transfers between devices  1.08 us (2%)
  between operations  0.74 us (1%)
    all_to_all x2, blocking collectives, local(): lax.all_to_all(jnp.broadcast_to(gram[None], (size, 1, 128)), axis, 0, 0)  41.3 us
    ppermute x2, starting transfers between devices, exchange(): lax.ppermute(to_other, 'gx', across)  8.03 us
    ppermute x2, starting transfers between devices, swap(): return (lax.ppermute(to_right, axis, up), lax.ppermute(to_left, axis, down))  5.33 us
    ppermute x2, starting transfers between devices, exchange(): lax.ppermute(to_partner, 'gx', chip)  4.41 us
  transfers between devices with their start and end apart: 6, of which 1 were waited for; matrix products, arithmetic and copies ran while one was open for 0% of the time, Pallas kernels for 0%

profile of v5, /device:TPU:1, one launch (start us, length us, event | category | flops | bytes accessed | tf_op | source)
XLA Modules:
  0.0 64.2 jit_solution(6136857141353481330)
XLA Ops:
  0.6 1.0 %shard_map.68 = (f32[4,4,8,256]{3,2,1,0:T(8,128)S(1)}, f32[4,4,8,256]{3,2,1,0:T(8,128)S(1)}, f32[3,4,8,256]{3,2,1,0:T(8,128)S(1)}, f32[19,8,256]{2,1,0:T(8,128)S(1)}, f32[19,8,256]{2,1,0:T(8,128)S(1)}) custom-call(f32[4,4,8,256]{3,2,1,0:T(8,128)} %source_in.1, s32[4,8,256]{2,1,0:T(8,128)} %labels_in.1, s32[4,8,256]{2,1,0:T(8,128)} %mask_in.1, ...), custom_call_target="tpu_custom_call" | custom-call | tf_op jit(solution)/shard_map/pallas_call | solution.py:358
  1.7 4.0 %collective-permute-start = (f32[19,8,256]{2,1,0:T(8,128)S(1)}, f32[19,8,256]{2,1,0:T(8,128)S(1)}, u32[]{:S(2)}, u32[]{:S(2)}) collective-permute-start(f32[19,8,256]{2,1,0:T(8,128)S(1)} %get-tuple-element.20), channel_id=1, source_target_pairs={{0,1},{1,2},{2,3},{3,4},{4,5},{5,6},{6,7},{7,8},{8,9},{9,10},{10,1... | collective-permute-start | bytes 466952 | tf_op jit(solution)/shard_map/ppermute | solution.py:330
  5.7 1.3 %collective-permute-start.1 = (f32[19,8,256]{2,1,0:T(8,128)S(1)}, f32[19,8,256]{2,1,0:T(8,128)S(1)}, u32[]{:S(2)}, u32[]{:S(2)}) collective-permute-start(f32[19,8,256]{2,1,0:T(8,128)S(1)} %get-tuple-element.21), channel_id=1, source_target_pairs={{1,0},{2,1},{3,2},{4,3},{5,4},{6,5},{7,6},{8,7},{9,8},{10,9},{11,1... | collective-permute-start | bytes 466952 | tf_op jit(solution)/shard_map/ppermute | solution.py:330
  7.1 4.4 %collective-permute-start.2 = (f32[30,8,256]{2,1,0:T(8,128)S(1)}, f32[30,8,256]{2,1,0:T(8,128)S(1)}, u32[]{:S(2)}, u32[]{:S(2)}) collective-permute-start(f32[30,8,256]{2,1,0:T(8,128)S(1)} %get-tuple-element.24), channel_id=1, source_target_pairs={{16,32},{32,16},{48,64},{64,48},{80,96},{96,80},{112,128},{128,112... | collective-permute-start | bytes 737288 | tf_op jit(solution)/shard_map/ppermute | solution.py:337
  11.5 2.3 %collective-permute-start.3 = (f32[30,8,256]{2,1,0:T(8,128)S(1)}, f32[30,8,256]{2,1,0:T(8,128)S(1)}, u32[]{:S(2)}, u32[]{:S(2)}) collective-permute-start(f32[30,8,256]{2,1,0:T(8,128)S(1)} %get-tuple-element.25), channel_id=1, source_target_pairs={{0,16},{16,0},{32,48},{48,32},{64,80},{80,64},{96,112},{112,96},{1... | collective-permute-start | bytes 737288 | tf_op jit(solution)/shard_map/ppermute | solution.py:337
  13.8 0.0 collective-permute-done.from_left
  13.8 0.0 collective-permute-done.1.from_right
  13.9 3.6 %collective-permute-start.4 = (f32[9,8,256]{2,1,0:T(8,128)S(1)}, f32[9,8,256]{2,1,0:T(8,128)S(1)}, u32[]{:S(2)}, u32[]{:S(2)}) collective-permute-start(f32[9,8,256]{2,1,0:T(8,128)S(1)} %get-tuple-element.26), channel_id=1, source_target_pairs={{16,32},{32,16},{48,64},{64,48},{80,96},{96,80},{112,128},{128,112... | collective-permute-start | bytes 221192 | tf_op jit(solution)/shard_map/ppermute | solution.py:337
  17.5 2.1 %collective-permute-start.5 = (f32[9,8,256]{2,1,0:T(8,128)S(1)}, f32[9,8,256]{2,1,0:T(8,128)S(1)}, u32[]{:S(2)}, u32[]{:S(2)}) collective-permute-start(f32[9,8,256]{2,1,0:T(8,128)S(1)} %get-tuple-element.27), channel_id=1, source_target_pairs={{0,16},{16,0},{32,48},{48,32},{64,80},{80,64},{96,112},{112,96},{1... | collective-permute-start | bytes 221192 | tf_op jit(solution)/shard_map/ppermute | solution.py:337
  19.6 0.0 collective-permute-done.4.far_corner
  19.6 1.1 %collective-permute-done.5.near_corner = f32[9,8,256]{2,1,0:T(8,128)S(1)} collective-permute-done((f32[9,8,256]{2,1,0:T(8,128)S(1)}, f32[9,8,256]{2,1,0:T(8,128)S(1)}, u32[]{:S(2)}, u32[]{:S(2)}) %collective-permute-start.5) | collective-permute-done | bytes 73760 | tf_op jit(solution)/shard_map/ppermute | solution.py:337
  20.7 0.0 collective-permute-done.2.far
  20.7 0.0 collective-permute-done.3.near
  20.7 1.1 %shard_map.71 = (f32[4,4,8,256]{3,2,1,0:T(8,128)S(1)}, f32[4,4,8,256]{3,2,1,0:T(8,128)S(1)}, f32[4,4,8,256]{3,2,1,0:T(8,128)S(1)}, f32[1,128]{1,0:T(1,128)S(1)}) custom-call(f32[4,4,8,256]{3,2,1,0:T(8,128)S(1)} %get-tuple-element.17.source, f32[4,4,8,256]{3,2,1,0:T(8,128)S(1)} %get-tuple-element.18.kcell, f32[3,4,8,256]{3,2,1,0:T(8,128)S(1)} %get-tuple-element.19.couple, ...), custom_call_target="tpu_custom_call" | custom-call | tf_op jit(solution)/shard_map/pallas_call | solution.py:342
  21.9 27.1 %all_to_all.10 = f32[32,1,128]{2,1,0:T(1,128)S(1)} all-to-all(f32[32,1,128]{2,1,0:T(1,128)S(1)} %broadcast_in_dim.7), channel_id=1, replica_groups=mesh['gx'=32,'gy'=16] {'gx'}, dimensions={0} | all-to-all | bytes 32768 | tf_op jit(solution)/shard_map/all_to_all | solution.py:387
  49.0 14.2 %all_to_all.11.gram = f32[16,1,128]{2,1,0:T(1,128)S(1)} all-to-all(f32[16,1,128]{2,1,0:T(1,128)S(1)} %broadcast_in_dim.16), channel_id=1, replica_groups=mesh['gx'=32,'gy'=16] {'gy'}, dimensions={0} | all-to-all | bytes 16384 | tf_op jit(solution)/shard_map/all_to_all | solution.py:387
  63.2 1.0 %shard_map.72 = (f32[4,4,8,256]{3,2,1,0:T(8,128)}, f32[4,4,8,256]{3,2,1,0:T(8,128)}) custom-call(f32[16,1,128]{2,1,0:T(1,128)S(1)} %all_to_all.11.gram, f32[4,4,8,256]{3,2,1,0:T(8,128)S(1)} %get-tuple-element.17.source, f32[4,4,8,256]{3,2,1,0:T(8,128)S(1)} %get-tuple-element.29.k1, f32[4,4,8,256]{3,2,1,0:T(8,128)S(1)} %get-tuple-element.30.k2, ...), custom_call_target="tpu_custom_call" | custom-call | tf_op jit(solution)/shard_map/pallas_call | solution.py:353
  (5 shorter events, 0.2 us)
Async XLA Ops:
  1.7 12.1 %collective-permute-start = (f32[19,8,256]{2,1,0:T(8,128)S(1)}, f32[19,8,256]{2,1,0:T(8,128)S(1)}, u32[]{:S(2)}, u32[]{:S(2)}) collective-permute-start(f32[19,8,256]{2,1,0:T(8,128)S(1)} %get-tuple-element.20), channel_id=1, source_target_pairs={{0,1},{1,2},{2,3},{3,4},{4,5},{5,6},{6,7},{7,8},{8,9},{9,10},{10,1... | collective-permute-start | bytes 466952 | tf_op jit(solution)/shard_map/ppermute | solution.py:330
  5.7 8.1 %collective-permute-start.1 = (f32[19,8,256]{2,1,0:T(8,128)S(1)}, f32[19,8,256]{2,1,0:T(8,128)S(1)}, u32[]{:S(2)}, u32[]{:S(2)}) collective-permute-start(f32[19,8,256]{2,1,0:T(8,128)S(1)} %get-tuple-element.21), channel_id=1, source_target_pairs={{1,0},{2,1},{3,2},{4,3},{5,4},{6,5},{7,6},{8,7},{9,8},{10,9},{11,1... | collective-permute-start | bytes 466952 | tf_op jit(solution)/shard_map/ppermute | solution.py:330
  7.1 13.6 %collective-permute-start.2 = (f32[30,8,256]{2,1,0:T(8,128)S(1)}, f32[30,8,256]{2,1,0:T(8,128)S(1)}, u32[]{:S(2)}, u32[]{:S(2)}) collective-permute-start(f32[30,8,256]{2,1,0:T(8,128)S(1)} %get-tuple-element.24), channel_id=1, source_target_pairs={{16,32},{32,16},{48,64},{64,48},{80,96},{96,80},{112,128},{128,112... | collective-permute-start | bytes 737288 | tf_op jit(solution)/shard_map/ppermute | solution.py:337
  11.5 9.2 %collective-permute-start.3 = (f32[30,8,256]{2,1,0:T(8,128)S(1)}, f32[30,8,256]{2,1,0:T(8,128)S(1)}, u32[]{:S(2)}, u32[]{:S(2)}) collective-permute-start(f32[30,8,256]{2,1,0:T(8,128)S(1)} %get-tuple-element.25), channel_id=1, source_target_pairs={{0,16},{16,0},{32,48},{48,32},{64,80},{80,64},{96,112},{112,96},{1... | collective-permute-start | bytes 737288 | tf_op jit(solution)/shard_map/ppermute | solution.py:337
  13.9 5.7 %collective-permute-start.4 = (f32[9,8,256]{2,1,0:T(8,128)S(1)}, f32[9,8,256]{2,1,0:T(8,128)S(1)}, u32[]{:S(2)}, u32[]{:S(2)}) collective-permute-start(f32[9,8,256]{2,1,0:T(8,128)S(1)} %get-tuple-element.26), channel_id=1, source_target_pairs={{16,32},{32,16},{48,64},{64,48},{80,96},{96,80},{112,128},{128,112... | collective-permute-start | bytes 221192 | tf_op jit(solution)/shard_map/ppermute | solution.py:337
  17.5 3.2 %collective-permute-start.5 = (f32[9,8,256]{2,1,0:T(8,128)S(1)}, f32[9,8,256]{2,1,0:T(8,128)S(1)}, u32[]{:S(2)}, u32[]{:S(2)}) collective-permute-start(f32[9,8,256]{2,1,0:T(8,128)S(1)} %get-tuple-element.27), channel_id=1, source_target_pairs={{0,16},{16,0},{32,48},{48,32},{64,80},{80,64},{96,112},{112,96},{1... | collective-permute-start | bytes 221192 | tf_op jit(solution)/shard_map/ppermute | solution.py:337

commit v6 on v5

--- a/solution.py
+++ b/solution.py
@@ -9,6 +9,7 @@
 SHIFT = (1.0, 0.5, 0.5, 1.0)
 WEIGHT = (0.8, 1.0, -1.0, -0.8)
 EPS = 1e-12
+FIRST = {"gx": 16, "gy": 10}
 F32 = jnp.float32
 VMEM = pl.BlockSpec(memory_space=pltpu.VMEM)
 HBM = pl.BlockSpec(memory_space=pltpu.HBM)
@@ -384,7 +385,10 @@
     )
     for axis in ("gx", "gy"):
         size = lax.axis_size(axis)
-        gram = lax.all_to_all(jnp.broadcast_to(gram[None], (size, 1, 128)), axis, 0, 0)
+        group = [(i + FIRST[axis]) % size for i in range(size)]
+        gram = lax.all_to_all(
+            jnp.broadcast_to(gram[None], (size, 1, 128)), axis, 0, 0, axis_index_groups=[group]
+        )
         if axis == "gx":
             gram = jnp.sum(gram, axis=0)
     return run_finish(gram, source, k1, k2, k3)

time: 64.5 us -> 54.2 us (0.84)
  blocking collectives: 41.3 us -> 30.4 us
    all_to_all x2, blocking collectives: 41.3 us -> 30.4 us  [local(): lax.all_to_all(jnp.broadcast_to(gram[None], (size, 1, 128)), axis, 0, 0,...]
where the time goes in v6:
time: 54.2 us; the launch traced here: 53.3 us
  blocking collectives  30.4 us (56%)
  starting transfers between devices  17.8 us (33%)
  Pallas kernels  3.22 us (6%)
  waiting for transfers between devices  1.08 us (2%)
  between operations  0.74 us (1%)
    all_to_all x2, blocking collectives, local(): lax.all_to_all(jnp.broadcast_to(gram[None], (size, 1, 128)), axis, 0, 0,...  30.4 us
    ppermute x2, starting transfers between devices, exchange(): lax.ppermute(to_other, 'gx', across)  8.03 us
    ppermute x2, starting transfers between devices, swap(): return (lax.ppermute(to_right, axis, up), lax.ppermute(to_left, axis, down))  5.33 us
    ppermute x2, starting transfers between devices, exchange(): lax.ppermute(to_partner, 'gx', chip)  4.41 us
    pallas_call x1, Pallas kernels, run_krylov(): call(krylov, 9, [four, four, four, (1, 128)], [(8, 4) + TILE, (3, 2) + TI...  1.13 us
  transfers between devices with their start and end apart: 6, of which 1 were waited for; matrix products, arithmetic and copies ran while one was open for 0% of the time, Pallas kernels for 0%

profile of v6, /device:TPU:1, one launch (start us, length us, event | category | flops | bytes accessed | tf_op | source)
XLA Modules:
  0.0 53.3 jit_solution(10674316136190769152)
XLA Ops:
  0.6 1.0 %shard_map.68 = (f32[4,4,8,256]{3,2,1,0:T(8,128)S(1)}, f32[4,4,8,256]{3,2,1,0:T(8,128)S(1)}, f32[3,4,8,256]{3,2,1,0:T(8,128)S(1)}, f32[19,8,256]{2,1,0:T(8,128)S(1)}, f32[19,8,256]{2,1,0:T(8,128)S(1)}) custom-call(f32[4,4,8,256]{3,2,1,0:T(8,128)} %source_in.1, s32[4,8,256]{2,1,0:T(8,128)} %labels_in.1, s32[4,8,256]{2,1,0:T(8,128)} %mask_in.1, ...), custom_call_target="tpu_custom_call" | custom-call | tf_op jit(solution)/shard_map/pallas_call | solution.py:359
  1.7 4.0 %collective-permute-start = (f32[19,8,256]{2,1,0:T(8,128)S(1)}, f32[19,8,256]{2,1,0:T(8,128)S(1)}, u32[]{:S(2)}, u32[]{:S(2)}) collective-permute-start(f32[19,8,256]{2,1,0:T(8,128)S(1)} %get-tuple-element.20), channel_id=1, source_target_pairs={{0,1},{1,2},{2,3},{3,4},{4,5},{5,6},{6,7},{7,8},{8,9},{9,10},{10,1... | collective-permute-start | bytes 466952 | tf_op jit(solution)/shard_map/ppermute | solution.py:331
  5.7 1.3 %collective-permute-start.1 = (f32[19,8,256]{2,1,0:T(8,128)S(1)}, f32[19,8,256]{2,1,0:T(8,128)S(1)}, u32[]{:S(2)}, u32[]{:S(2)}) collective-permute-start(f32[19,8,256]{2,1,0:T(8,128)S(1)} %get-tuple-element.21), channel_id=1, source_target_pairs={{1,0},{2,1},{3,2},{4,3},{5,4},{6,5},{7,6},{8,7},{9,8},{10,9},{11,1... | collective-permute-start | bytes 466952 | tf_op jit(solution)/shard_map/ppermute | solution.py:331
  7.1 4.4 %collective-permute-start.2 = (f32[30,8,256]{2,1,0:T(8,128)S(1)}, f32[30,8,256]{2,1,0:T(8,128)S(1)}, u32[]{:S(2)}, u32[]{:S(2)}) collective-permute-start(f32[30,8,256]{2,1,0:T(8,128)S(1)} %get-tuple-element.24), channel_id=1, source_target_pairs={{16,32},{32,16},{48,64},{64,48},{80,96},{96,80},{112,128},{128,112... | collective-permute-start | bytes 737288 | tf_op jit(solution)/shard_map/ppermute | solution.py:338
  11.5 2.3 %collective-permute-start.3 = (f32[30,8,256]{2,1,0:T(8,128)S(1)}, f32[30,8,256]{2,1,0:T(8,128)S(1)}, u32[]{:S(2)}, u32[]{:S(2)}) collective-permute-start(f32[30,8,256]{2,1,0:T(8,128)S(1)} %get-tuple-element.25), channel_id=1, source_target_pairs={{0,16},{16,0},{32,48},{48,32},{64,80},{80,64},{96,112},{112,96},{1... | collective-permute-start | bytes 737288 | tf_op jit(solution)/shard_map/ppermute | solution.py:338
  13.8 0.0 collective-permute-done.from_left
  13.8 0.0 collective-permute-done.1.from_right
  13.9 3.6 %collective-permute-start.4 = (f32[9,8,256]{2,1,0:T(8,128)S(1)}, f32[9,8,256]{2,1,0:T(8,128)S(1)}, u32[]{:S(2)}, u32[]{:S(2)}) collective-permute-start(f32[9,8,256]{2,1,0:T(8,128)S(1)} %get-tuple-element.26), channel_id=1, source_target_pairs={{16,32},{32,16},{48,64},{64,48},{80,96},{96,80},{112,128},{128,112... | collective-permute-start | bytes 221192 | tf_op jit(solution)/shard_map/ppermute | solution.py:338
  17.5 2.1 %collective-permute-start.5 = (f32[9,8,256]{2,1,0:T(8,128)S(1)}, f32[9,8,256]{2,1,0:T(8,128)S(1)}, u32[]{:S(2)}, u32[]{:S(2)}) collective-permute-start(f32[9,8,256]{2,1,0:T(8,128)S(1)} %get-tuple-element.27), channel_id=1, source_target_pairs={{0,16},{16,0},{32,48},{48,32},{64,80},{80,64},{96,112},{112,96},{1... | collective-permute-start | bytes 221192 | tf_op jit(solution)/shard_map/ppermute | solution.py:338
  19.6 0.0 collective-permute-done.4.far_corner
  19.6 1.1 %collective-permute-done.5.near_corner = f32[9,8,256]{2,1,0:T(8,128)S(1)} collective-permute-done((f32[9,8,256]{2,1,0:T(8,128)S(1)}, f32[9,8,256]{2,1,0:T(8,128)S(1)}, u32[]{:S(2)}, u32[]{:S(2)}) %collective-permute-start.5) | collective-permute-done | bytes 73760 | tf_op jit(solution)/shard_map/ppermute | solution.py:338
  20.7 0.0 collective-permute-done.2.far
  20.7 0.0 collective-permute-done.3.near
  20.7 1.1 %shard_map.71 = (f32[4,4,8,256]{3,2,1,0:T(8,128)S(1)}, f32[4,4,8,256]{3,2,1,0:T(8,128)S(1)}, f32[4,4,8,256]{3,2,1,0:T(8,128)S(1)}, f32[1,128]{1,0:T(1,128)S(1)}) custom-call(f32[4,4,8,256]{3,2,1,0:T(8,128)S(1)} %get-tuple-element.17.source, f32[4,4,8,256]{3,2,1,0:T(8,128)S(1)} %get-tuple-element.18.kcell, f32[3,4,8,256]{3,2,1,0:T(8,128)S(1)} %get-tuple-element.19.couple, ...), custom_call_target="tpu_custom_call" | custom-call | tf_op jit(solution)/shard_map/pallas_call | solution.py:343
  21.9 19.7 %all_to_all.10 = f32[32,1,128]{2,1,0:T(1,128)S(1)} all-to-all(f32[32,1,128]{2,1,0:T(1,128)S(1)} %broadcast_in_dim.7), channel_id=1, replica_groups={{256,272,288,304,320,336,352,368,384,400,416,432,448,464,480,496,0,16,3..., dimensions={0} | all-to-all | bytes 32768 | tf_op jit(solution)/shard_map/all_to_all | solution.py:389
  41.6 10.8 %all_to_all.11.gram = f32[16,1,128]{2,1,0:T(1,128)S(1)} all-to-all(f32[16,1,128]{2,1,0:T(1,128)S(1)} %broadcast_in_dim.16), channel_id=1, replica_groups={{10,11,12,13,14,15,0,1,2,3,4,5,6,7,8,9},{26,27,28,29,30,31,16,17,18,19,..., dimensions={0} | all-to-all | bytes 16384 | tf_op jit(solution)/shard_map/all_to_all | solution.py:389
  52.4 1.0 %shard_map.72 = (f32[4,4,8,256]{3,2,1,0:T(8,128)}, f32[4,4,8,256]{3,2,1,0:T(8,128)}) custom-call(f32[16,1,128]{2,1,0:T(1,128)S(1)} %all_to_all.11.gram, f32[4,4,8,256]{3,2,1,0:T(8,128)S(1)} %get-tuple-element.17.source, f32[4,4,8,256]{3,2,1,0:T(8,128)S(1)} %get-tuple-element.29.k1, f32[4,4,8,256]{3,2,1,0:T(8,128)S(1)} %get-tuple-element.30.k2, ...), custom_call_target="tpu_custom_call" | custom-call | tf_op jit(solution)/shard_map/pallas_call | solution.py:354
  (5 shorter events, 0.2 us)
Async XLA Ops:
  1.7 12.1 %collective-permute-start = (f32[19,8,256]{2,1,0:T(8,128)S(1)}, f32[19,8,256]{2,1,0:T(8,128)S(1)}, u32[]{:S(2)}, u32[]{:S(2)}) collective-permute-start(f32[19,8,256]{2,1,0:T(8,128)S(1)} %get-tuple-element.20), channel_id=1, source_target_pairs={{0,1},{1,2},{2,3},{3,4},{4,5},{5,6},{6,7},{7,8},{8,9},{9,10},{10,1... | collective-permute-start | bytes 466952 | tf_op jit(solution)/shard_map/ppermute | solution.py:331
  5.7 8.1 %collective-permute-start.1 = (f32[19,8,256]{2,1,0:T(8,128)S(1)}, f32[19,8,256]{2,1,0:T(8,128)S(1)}, u32[]{:S(2)}, u32[]{:S(2)}) collective-permute-start(f32[19,8,256]{2,1,0:T(8,128)S(1)} %get-tuple-element.21), channel_id=1, source_target_pairs={{1,0},{2,1},{3,2},{4,3},{5,4},{6,5},{7,6},{8,7},{9,8},{10,9},{11,1... | collective-permute-start | bytes 466952 | tf_op jit(solution)/shard_map/ppermute | solution.py:331
  7.1 13.6 %collective-permute-start.2 = (f32[30,8,256]{2,1,0:T(8,128)S(1)}, f32[30,8,256]{2,1,0:T(8,128)S(1)}, u32[]{:S(2)}, u32[]{:S(2)}) collective-permute-start(f32[30,8,256]{2,1,0:T(8,128)S(1)} %get-tuple-element.24), channel_id=1, source_target_pairs={{16,32},{32,16},{48,64},{64,48},{80,96},{96,80},{112,128},{128,112... | collective-permute-start | bytes 737288 | tf_op jit(solution)/shard_map/ppermute | solution.py:338
  11.5 9.2 %collective-permute-start.3 = (f32[30,8,256]{2,1,0:T(8,128)S(1)}, f32[30,8,256]{2,1,0:T(8,128)S(1)}, u32[]{:S(2)}, u32[]{:S(2)}) collective-permute-start(f32[30,8,256]{2,1,0:T(8,128)S(1)} %get-tuple-element.25), channel_id=1, source_target_pairs={{0,16},{16,0},{32,48},{48,32},{64,80},{80,64},{96,112},{112,96},{1... | collective-permute-start | bytes 737288 | tf_op jit(solution)/shard_map/ppermute | solution.py:338
  13.9 5.7 %collective-permute-start.4 = (f32[9,8,256]{2,1,0:T(8,128)S(1)}, f32[9,8,256]{2,1,0:T(8,128)S(1)}, u32[]{:S(2)}, u32[]{:S(2)}) collective-permute-start(f32[9,8,256]{2,1,0:T(8,128)S(1)} %get-tuple-element.26), channel_id=1, source_target_pairs={{16,32},{32,16},{48,64},{64,48},{80,96},{96,80},{112,128},{128,112... | collective-permute-start | bytes 221192 | tf_op jit(solution)/shard_map/ppermute | solution.py:338
  17.5 3.2 %collective-permute-start.5 = (f32[9,8,256]{2,1,0:T(8,128)S(1)}, f32[9,8,256]{2,1,0:T(8,128)S(1)}, u32[]{:S(2)}, u32[]{:S(2)}) collective-permute-start(f32[9,8,256]{2,1,0:T(8,128)S(1)} %get-tuple-element.27), channel_id=1, source_target_pairs={{0,16},{16,0},{32,48},{48,32},{64,80},{80,64},{96,112},{112,96},{1... | collective-permute-start | bytes 221192 | tf_op jit(solution)/shard_map/ppermute | solution.py:338

commit v7 on v6

--- a/solution.py
+++ b/solution.py
@@ -9,12 +9,12 @@
 SHIFT = (1.0, 0.5, 0.5, 1.0)
 WEIGHT = (0.8, 1.0, -1.0, -0.8)
 EPS = 1e-12
-FIRST = {"gx": 16, "gy": 10}
+FIRST = {"gx": 17, "gy": 10}
 F32 = jnp.float32
 VMEM = pl.BlockSpec(memory_space=pltpu.VMEM)
 HBM = pl.BlockSpec(memory_space=pltpu.HBM)
 TILE = (8, 256)
-Y_TILES = 19
+Y_TILES = 15
 X_TILES = 30
 CORNER_TILES = 9
 PAIRS = [(i, j) for i in range(4) for j in range(i, 4)]
@@ -38,11 +38,21 @@
         c.start()
     row = rows()
 
-    def faces(f, ref):
-        for k in range(2):
-            a, b = ref[f % 4, 2 * k], ref[f % 4, 2 * k + 1]
-            to_right[2 * f + k] = jnp.where(row >= 5, a, roll(b, -3))
-            to_left[2 * f + k] = jnp.where(row < 3, a, roll(b, 3))
+    def faces(ref):
+        for g in range(2):
+            base = (0 if ref is source else 6) + 3 * g
+            units = [ref[2 * g + i // 4, i % 4] for i in range(8)]
+            for k in range(3):
+                a, b = units[2 * k], units[2 * k + 1]
+                if k < 2:
+                    c = units[6 + k]
+                    right, left = roll(c, -6), roll(c, 6)
+                else:
+                    c, d = units[6], units[7]
+                    right = jnp.where(row == 0, roll(c, -5), roll(d, -4))
+                    left = jnp.where(row == 7, roll(c, 5), roll(d, 4))
+                to_right[base + k] = jnp.where(row >= 5, a, jnp.where(row >= 2, roll(b, -3), right))
+                to_left[base + k] = jnp.where(row < 3, a, jnp.where(row < 6, roll(b, 3), left))
 
     copies[0].wait()
     copies[1].wait()
@@ -52,11 +62,9 @@
             t = PHASE[f]
             base = jnp.where(phase == 0, t[0], jnp.where(phase == 1, t[1], t[2]))
             kcell[f, x] = base * conduct[f, x].astype(F32)
-    for f in range(4):
-        faces(4 + f, kcell)
+    faces(kcell)
     copies[2].wait()
-    for f in range(4):
-        faces(f, source)
+    faces(source)
     copies[3].wait()
     copies[4].wait()
     for x in range(4):
@@ -68,8 +76,8 @@
         for x in range(1, 4):
             right = jnp.where(row >= 8 - 2 * x, right, roll(couple[f, x], -2 * x))
             left = jnp.where(row < 2 * x, left, roll(couple[f, x], 2 * x))
-        to_right[16 + f] = right
-        to_left[16 + f] = left
+        to_right[12 + f] = right
+        to_left[12 + f] = left
 
 
 def columns_from_partner():
@@ -91,12 +99,20 @@
     row = rows()
     for f in range(8):
         for x in range(4):
-            k, b = 2 * f + x // 2, 3 * (x % 2)
-            left, right = roll(from_left[k], b), roll(from_right[k], -b)
+            base, unit = 3 * (f // 2), 4 * (f % 2) + x
+            if unit < 6:
+                k, by = base + unit // 2, 3 * (unit % 2)
+                left, right = roll(from_left[k], by), roll(from_right[k], -by)
+            elif unit == 6:
+                left = jnp.where(row == 5, roll(from_left[base + 2], 5), roll(from_left[base], 6))
+                right = jnp.where(row == 2, roll(from_right[base + 2], -5), roll(from_right[base], -6))
+            else:
+                left = jnp.where(row == 5, roll(from_left[base + 2], 4), roll(from_left[base + 1], 6))
+                right = jnp.where(row == 2, roll(from_right[base + 2], -4), roll(from_right[base + 1], -6))
             rim[f, x] = jnp.where(row < 4, right, left)
     for f in range(3):
         for x in range(4):
-            left, right = roll(from_left[16 + f], 2 * x), roll(from_right[16 + f], -2 * x)
+            left, right = roll(from_left[12 + f], 2 * x), roll(from_right[12 + f], -2 * x)
             crim[f, x] = jnp.where(row < 4, right, left)
     own = columns_from_partner()
     for out, order in ((to_partner, own[:2]), (to_other, own[:1:-1])):

time: 54.2 us -> 54 us (level)
  transfers between devices with their start and end apart: 6 -> 6, of which waited for: 1 -> 2; matrix products, arithmetic and copies ran while one was open for 0% -> 0% of each run, Pallas kernels for 0% -> 0%
where the time goes in v7:
time: 54 us; the launch traced here: 53 us
  blocking collectives  30.3 us (56%)
  starting transfers between devices  17.5 us (32%)
  Pallas kernels  3.23 us (6%)
  waiting for transfers between devices  1.24 us (2%)
  between operations  0.73 us (1%)
    all_to_all x2, blocking collectives, local(): lax.all_to_all(jnp.broadcast_to(gram[None], (size, 1, 128)), axis, 0, 0,...  30.3 us
    ppermute x2, starting transfers between devices, exchange(): lax.ppermute(to_other, 'gx', across)  7.9 us
    ppermute x2, starting transfers between devices, swap(): return (lax.ppermute(to_right, axis, up), lax.ppermute(to_left, axis, down))  5.33 us
    ppermute x2, starting transfers between devices, exchange(): lax.ppermute(to_partner, 'gx', chip)  4.26 us
    pallas_call x1, Pallas kernels, run_krylov(): call(krylov, 9, [four, four, four, (1, 128)], [(8, 4) + TILE, (3, 2) + TI...  1.13 us
  transfers between devices with their start and end apart: 6, of which 2 were waited for; matrix products, arithmetic and copies ran while one was open for 0% of the time, Pallas kernels for 0%

profile of v7, /device:TPU:1, one launch (start us, length us, event | category | flops | bytes accessed | tf_op | source)
XLA Modules:
  0.0 53.0 jit_solution(5149688507213241367)
XLA Ops:
  0.6 1.0 %shard_map.68 = (f32[4,4,8,256]{3,2,1,0:T(8,128)S(1)}, f32[4,4,8,256]{3,2,1,0:T(8,128)S(1)}, f32[3,4,8,256]{3,2,1,0:T(8,128)S(1)}, f32[15,8,256]{2,1,0:T(8,128)S(1)}, f32[15,8,256]{2,1,0:T(8,128)S(1)}) custom-call(f32[4,4,8,256]{3,2,1,0:T(8,128)} %source_in.1, s32[4,8,256]{2,1,0:T(8,128)} %labels_in.1, s32[4,8,256]{2,1,0:T(8,128)} %mask_in.1, ...), custom_call_target="tpu_custom_call" | custom-call | tf_op jit(solution)/shard_map/pallas_call | solution.py:375
  1.7 4.0 %collective-permute-start = (f32[15,8,256]{2,1,0:T(8,128)S(1)}, f32[15,8,256]{2,1,0:T(8,128)S(1)}, u32[]{:S(2)}, u32[]{:S(2)}) collective-permute-start(f32[15,8,256]{2,1,0:T(8,128)S(1)} %get-tuple-element.20), channel_id=1, source_target_pairs={{0,1},{1,2},{2,3},{3,4},{4,5},{5,6},{6,7},{7,8},{8,9},{9,10},{10,1... | collective-permute-start | bytes 368648 | tf_op jit(solution)/shard_map/ppermute | solution.py:347
  5.7 1.3 %collective-permute-start.1 = (f32[15,8,256]{2,1,0:T(8,128)S(1)}, f32[15,8,256]{2,1,0:T(8,128)S(1)}, u32[]{:S(2)}, u32[]{:S(2)}) collective-permute-start(f32[15,8,256]{2,1,0:T(8,128)S(1)} %get-tuple-element.21), channel_id=1, source_target_pairs={{1,0},{2,1},{3,2},{4,3},{5,4},{6,5},{7,6},{8,7},{9,8},{10,9},{11,1... | collective-permute-start | bytes 368648 | tf_op jit(solution)/shard_map/ppermute | solution.py:347
  7.1 4.4 %collective-permute-start.2 = (f32[30,8,256]{2,1,0:T(8,128)S(1)}, f32[30,8,256]{2,1,0:T(8,128)S(1)}, u32[]{:S(2)}, u32[]{:S(2)}) collective-permute-start(f32[30,8,256]{2,1,0:T(8,128)S(1)} %get-tuple-element.24), channel_id=1, source_target_pairs={{16,32},{32,16},{48,64},{64,48},{80,96},{96,80},{112,128},{128,112... | collective-permute-start | bytes 737288 | tf_op jit(solution)/shard_map/ppermute | solution.py:354
  11.5 2.3 %collective-permute-start.3 = (f32[30,8,256]{2,1,0:T(8,128)S(1)}, f32[30,8,256]{2,1,0:T(8,128)S(1)}, u32[]{:S(2)}, u32[]{:S(2)}) collective-permute-start(f32[30,8,256]{2,1,0:T(8,128)S(1)} %get-tuple-element.25), channel_id=1, source_target_pairs={{0,16},{16,0},{32,48},{48,32},{64,80},{80,64},{96,112},{112,96},{1... | collective-permute-start | bytes 737288 | tf_op jit(solution)/shard_map/ppermute | solution.py:354
  13.8 0.0 collective-permute-done.from_left
  13.8 0.0 collective-permute-done.1.from_right
  13.8 0.1 shard_map.69
  13.9 3.5 %collective-permute-start.4 = (f32[9,8,256]{2,1,0:T(8,128)S(1)}, f32[9,8,256]{2,1,0:T(8,128)S(1)}, u32[]{:S(2)}, u32[]{:S(2)}) collective-permute-start(f32[9,8,256]{2,1,0:T(8,128)S(1)} %get-tuple-element.26), channel_id=1, source_target_pairs={{16,32},{32,16},{48,64},{64,48},{80,96},{96,80},{112,128},{128,112... | collective-permute-start | bytes 221192 | tf_op jit(solution)/shard_map/ppermute | solution.py:354
  17.4 1.9 %collective-permute-start.5 = (f32[9,8,256]{2,1,0:T(8,128)S(1)}, f32[9,8,256]{2,1,0:T(8,128)S(1)}, u32[]{:S(2)}, u32[]{:S(2)}) collective-permute-start(f32[9,8,256]{2,1,0:T(8,128)S(1)} %get-tuple-element.27), channel_id=1, source_target_pairs={{0,16},{16,0},{32,48},{48,32},{64,80},{80,64},{96,112},{112,96},{1... | collective-permute-start | bytes 221192 | tf_op jit(solution)/shard_map/ppermute | solution.py:354
  19.4 0.2 collective-permute-done.4.far_corner
  19.6 1.0 %collective-permute-done.5.near_corner = f32[9,8,256]{2,1,0:T(8,128)S(1)} collective-permute-done((f32[9,8,256]{2,1,0:T(8,128)S(1)}, f32[9,8,256]{2,1,0:T(8,128)S(1)}, u32[]{:S(2)}, u32[]{:S(2)}) %collective-permute-start.5) | collective-permute-done | bytes 73760 | tf_op jit(solution)/shard_map/ppermute | solution.py:354
  20.6 0.0 collective-permute-done.2.far
  20.6 0.0 collective-permute-done.3.near
  20.6 1.1 %shard_map.71 = (f32[4,4,8,256]{3,2,1,0:T(8,128)S(1)}, f32[4,4,8,256]{3,2,1,0:T(8,128)S(1)}, f32[4,4,8,256]{3,2,1,0:T(8,128)S(1)}, f32[1,128]{1,0:T(1,128)S(1)}) custom-call(f32[4,4,8,256]{3,2,1,0:T(8,128)S(1)} %get-tuple-element.17.source, f32[4,4,8,256]{3,2,1,0:T(8,128)S(1)} %get-tuple-element.18.kcell, f32[3,4,8,256]{3,2,1,0:T(8,128)S(1)} %get-tuple-element.19.couple, ...), custom_call_target="tpu_custom_call" | custom-call | tf_op jit(solution)/shard_map/pallas_call | solution.py:359
  21.8 18.9 %all_to_all.10 = f32[32,1,128]{2,1,0:T(1,128)S(1)} all-to-all(f32[32,1,128]{2,1,0:T(1,128)S(1)} %broadcast_in_dim.7), channel_id=1, replica_groups={{272,288,304,320,336,352,368,384,400,416,432,448,464,480,496,0,16,32,48..., dimensions={0} | all-to-all | bytes 32768 | tf_op jit(solution)/shard_map/all_to_all | solution.py:405
  40.7 11.4 %all_to_all.11.gram = f32[16,1,128]{2,1,0:T(1,128)S(1)} all-to-all(f32[16,1,128]{2,1,0:T(1,128)S(1)} %broadcast_in_dim.16), channel_id=1, replica_groups={{10,11,12,13,14,15,0,1,2,3,4,5,6,7,8,9},{26,27,28,29,30,31,16,17,18,19,..., dimensions={0} | all-to-all | bytes 16384 | tf_op jit(solution)/shard_map/all_to_all | solution.py:405
  52.1 1.0 %shard_map.72 = (f32[4,4,8,256]{3,2,1,0:T(8,128)}, f32[4,4,8,256]{3,2,1,0:T(8,128)}) custom-call(f32[16,1,128]{2,1,0:T(1,128)S(1)} %all_to_all.11.gram, f32[4,4,8,256]{3,2,1,0:T(8,128)S(1)} %get-tuple-element.17.source, f32[4,4,8,256]{3,2,1,0:T(8,128)S(1)} %get-tuple-element.29.k1, f32[4,4,8,256]{3,2,1,0:T(8,128)S(1)} %get-tuple-element.30.k2, ...), custom_call_target="tpu_custom_call" | custom-call | tf_op jit(solution)/shard_map/pallas_call | solution.py:370
  (4 shorter events, 0.1 us)
Async XLA Ops:
  1.7 12.1 %collective-permute-start = (f32[15,8,256]{2,1,0:T(8,128)S(1)}, f32[15,8,256]{2,1,0:T(8,128)S(1)}, u32[]{:S(2)}, u32[]{:S(2)}) collective-permute-start(f32[15,8,256]{2,1,0:T(8,128)S(1)} %get-tuple-element.20), channel_id=1, source_target_pairs={{0,1},{1,2},{2,3},{3,4},{4,5},{5,6},{6,7},{7,8},{8,9},{9,10},{10,1... | collective-permute-start | bytes 368648 | tf_op jit(solution)/shard_map/ppermute | solution.py:347
  5.7 8.1 %collective-permute-start.1 = (f32[15,8,256]{2,1,0:T(8,128)S(1)}, f32[15,8,256]{2,1,0:T(8,128)S(1)}, u32[]{:S(2)}, u32[]{:S(2)}) collective-permute-start(f32[15,8,256]{2,1,0:T(8,128)S(1)} %get-tuple-element.21), channel_id=1, source_target_pairs={{1,0},{2,1},{3,2},{4,3},{5,4},{6,5},{7,6},{8,7},{9,8},{10,9},{11,1... | collective-permute-start | bytes 368648 | tf_op jit(solution)/shard_map/ppermute | solution.py:347
  7.1 13.5 %collective-permute-start.2 = (f32[30,8,256]{2,1,0:T(8,128)S(1)}, f32[30,8,256]{2,1,0:T(8,128)S(1)}, u32[]{:S(2)}, u32[]{:S(2)}) collective-permute-start(f32[30,8,256]{2,1,0:T(8,128)S(1)} %get-tuple-element.24), channel_id=1, source_target_pairs={{16,32},{32,16},{48,64},{64,48},{80,96},{96,80},{112,128},{128,112... | collective-permute-start | bytes 737288 | tf_op jit(solution)/shard_map/ppermute | solution.py:354
  11.5 9.1 %collective-permute-start.3 = (f32[30,8,256]{2,1,0:T(8,128)S(1)}, f32[30,8,256]{2,1,0:T(8,128)S(1)}, u32[]{:S(2)}, u32[]{:S(2)}) collective-permute-start(f32[30,8,256]{2,1,0:T(8,128)S(1)} %get-tuple-element.25), channel_id=1, source_target_pairs={{0,16},{16,0},{32,48},{48,32},{64,80},{80,64},{96,112},{112,96},{1... | collective-permute-start | bytes 737288 | tf_op jit(solution)/shard_map/ppermute | solution.py:354
  13.9 5.7 %collective-permute-start.4 = (f32[9,8,256]{2,1,0:T(8,128)S(1)}, f32[9,8,256]{2,1,0:T(8,128)S(1)}, u32[]{:S(2)}, u32[]{:S(2)}) collective-permute-start(f32[9,8,256]{2,1,0:T(8,128)S(1)} %get-tuple-element.26), channel_id=1, source_target_pairs={{16,32},{32,16},{48,64},{64,48},{80,96},{96,80},{112,128},{128,112... | collective-permute-start | bytes 221192 | tf_op jit(solution)/shard_map/ppermute | solution.py:354
  17.4 3.2 %collective-permute-start.5 = (f32[9,8,256]{2,1,0:T(8,128)S(1)}, f32[9,8,256]{2,1,0:T(8,128)S(1)}, u32[]{:S(2)}, u32[]{:S(2)}) collective-permute-start(f32[9,8,256]{2,1,0:T(8,128)S(1)} %get-tuple-element.27), channel_id=1, source_target_pairs={{0,16},{16,0},{32,48},{48,32},{64,80},{80,64},{96,112},{112,96},{1... | collective-permute-start | bytes 221192 | tf_op jit(solution)/shard_map/ppermute | solution.py:354
